TPU v7x, 32 devices: a whole 2x2x4 slice. The times are simulated.
32 devices in a mesh: ctx: 8 (over z, y), head: 4 (over x, core).
Axes of the slice: x: 2, y: 2, z: 4, core: 2. Of those that a mesh axis runs over, the one named last changes fastest.
Arguments:
- queries: bfloat16 [2048, 32, 128], P('ctx', 'head'), may hold values from -6 to 6
- key_states: bfloat16 [2048, 4, 128], P('ctx', 'head'), may hold values from -6 to 6
- value_states: bfloat16 [2048, 4, 128], P('ctx', 'head'), may hold values from -6 to 6
- doc_lengths: int32 [8], replicated, may hold values from 1 to 1792, 2048 in all
- grad_attended: bfloat16 [2048, 4096], P(('ctx', 'head')), may hold values from -6 to 6
Outputs:
- attended: bfloat16 [2048, 4096], P(('ctx', 'head'))
- grad_queries: bfloat16 [2048, 32, 128], P('ctx', 'head')
- grad_keys: bfloat16 [2048, 4, 128], P('ctx', 'head')
- grad_values: bfloat16 [2048, 4, 128], P('ctx', 'head')
All inputs are finite; a program needn't handle non-finite values.
Results may differ from a plain program's by a relative error of at most 0.022.
Values may be sent and summed in bfloat16 or wider, within the bound.
No kernel may reach another device: no remote copies, remote signals or barrier semaphores. Data moves between devices by JAX's collectives and lax.ppermute only.
A program may use at most 64 MiB of HBM per device.

v0:
```python
import functools
import math

import jax
import jax.numpy as jnp
from jax import lax
from jax.experimental import pallas as pl
from jax.experimental.pallas import tpu as pltpu
from jax.sharding import PartitionSpec as P

DOC_MOST = 1792
NEG_FILL = -1e30
TILE = 256
CHUNK = 128
LOG2_E = 1.4426950408889634
SMALL_VMEM = 8 * 1024 * 1024
KERNEL_VMEM = 16 * 1024 * 1024


def dot(a, b):
    return jnp.dot(a, b, preferred_element_type=jnp.float32)


def dot_nt(a, b):
    return lax.dot_general(a, b, (((1,), (1,)), ((), ())), preferred_element_type=jnp.float32)


def unit(size):
    rows = lax.broadcasted_iota(jnp.int32, (size, size), 0)
    return (rows == lax.broadcasted_iota(jnp.int32, (size, size), 1)).astype(jnp.bfloat16)


def twice(column):
    return jnp.concatenate([column, column], axis=1)


def starts_in(doc_ref, positions):
    found = jnp.zeros_like(positions)
    for i in range(doc_ref.shape[0]):
        found = jnp.where(positions >= doc_ref[i], doc_ref[i], found)
    return found


def here(tok, back, whole):
    ctx = lax.axis_index("ctx")
    parity = lax.rem(ctx, 2)
    last = ctx // 2 if whole else back
    base = 0 if whole else (ctx - parity - 2 * back) * tok
    return parity, last, base, 2 * last + parity


def back_tile(i, slot, chunk, width, refs):
    q_cols, do_rows, do_cols, keys, values, scores, top, delta, dq_acc, d_blocks = refs
    at = pl.ds(pl.multiple_of(i * TILE, TILE), TILE)
    probs = jnp.exp2(scores[chunk, i] - twice(top[chunk]))
    d_probs = dot_nt(do_rows[chunk], values[at, 0:width])
    d_scores = (probs * (d_probs - twice(delta[chunk]))).astype(jnp.bfloat16)
    dq_acc[chunk] += dot(d_scores, keys[at, :])
    d_blocks[slot, 0:width, :] += dot(q_cols[chunk], d_scores)
    d_blocks[slot, width:, :] += dot(do_cols[chunk], probs.astype(jnp.bfloat16))


def put(d_blocks, mine, other, mine_ref, other_ref, width, scale):
    mine_ref[0:width, :] = d_blocks[mine, 0:width, :] * scale
    mine_ref[width:, :] = d_blocks[mine, width:, :]
    other_ref[0:width, :] = (d_blocks[other, 0:width, :] * scale).astype(jnp.bfloat16)
    other_ref[width:, :] = d_blocks[other, width:, :].astype(jnp.bfloat16)


def attention_kernel(
    doc_ref,
    q_rows,
    q_cols,
    do_rows,
    do_cols,
    own_ref,
    near_ref,
    *refs,
    back,
    whole,
    ranks,
    heads,
    width,
    scale,
):
    arrived, far, refs = refs[:back], refs[back : 2 * back], refs[2 * back :]
    out_parts, refs = refs[:ranks], refs[ranks:]
    (lows_ref, scores, top, delta, keys, values, dq_acc), refs = refs[:7], refs[7:]
    d_refs, (o_ref, accum, d_blocks) = refs[:-3], refs[-3:]
    tok = own_ref.shape[0] // 2
    part_rows = tok // ranks
    rank = lax.axis_index("head")
    parity, last, base, own = here(tok, back, whole)
    cut = 2 * (last - 1)
    ones = jnp.ones((width, width), jnp.bfloat16)

    values[:, width:] = jnp.ones_like(values[:, width:])
    for k in range(back + 1):
        pair = last ^ k if whole else last - k
        mine, other = (own_ref, near_ref) if k == 0 else (arrived[k - 1], far[k - 1])
        for ref, place in ((mine, 2 * pair + parity), (other, 2 * pair + 1 - parity)):
            at = pl.ds(pl.multiple_of(place * tok, tok), tok)
            keys[at, :] = ref[0:tok, :]
            values[at, 0:width] = ref[tok:, :]
    d_blocks[...] = jnp.zeros_like(d_blocks)
    top[...] = jnp.full_like(top, NEG_FILL)
    dq_acc[...] = jnp.zeros_like(dq_acc)

    def chunk_step(chunk, carry):
        rows_at = pl.ds(pl.multiple_of(chunk * CHUNK, CHUNK), CHUNK)
        t_first = base + own * TILE + chunk * CHUNK
        t_last = t_first + CHUNK - 1
        t_col = t_first + lax.broadcasted_iota(jnp.int32, (CHUNK, width), 0)
        start_col = starts_in(doc_ref, t_col)
        low = jnp.maximum(starts_in(doc_ref, t_first) - base, 0) // TILE
        lows_ref[chunk] = low
        clear = jnp.clip((starts_in(doc_ref, t_last) - base + TILE - 1) // TILE, low, own)

        def score_tile(i, masked):
            at = pl.ds(pl.multiple_of(i * TILE, TILE), TILE)
            tile = dot_nt(q_rows[chunk], keys[at, :]) * (scale * LOG2_E)
            if masked:
                s_row = base + i * TILE + lax.broadcasted_iota(jnp.int32, (CHUNK, TILE), 1)
                live = (s_row >= twice(start_col)) & (s_row <= twice(t_col))
                tile = jnp.concatenate(
                    [
                        jnp.where(live, tile[j * CHUNK : (j + 1) * CHUNK], NEG_FILL)
                        for j in range(heads)
                    ],
                    axis=0,
                )
            scores[chunk, i] = tile
            top[chunk] = jnp.maximum(top[chunk], jnp.maximum(tile[:, :width], tile[:, width:]))

        def edge_step(n, carry):
            score_tile(jnp.where(n < clear - low, low + n, own), True)
            return carry

        def inner_step(i, carry):
            score_tile(i, False)
            return carry

        lax.fori_loop(0, clear - low + 1, edge_step, 0)
        lax.fori_loop(clear, own, inner_step, 0)
        top[chunk] = jnp.broadcast_to(jnp.max(top[chunk], axis=1, keepdims=True), top.shape[1:])
        accum[...] = jnp.zeros_like(accum)

        def weigh_step(i, carry):
            at = pl.ds(pl.multiple_of(i * TILE, TILE), TILE)
            weights = jnp.exp2(scores[chunk, i] - twice(top[chunk])).astype(jnp.bfloat16)
            accum[...] += dot(weights, values[at, :])
            return carry

        lax.fori_loop(low, own + 1, weigh_step, 0)
        total = accum[:, width:]
        out = (accum[:, 0:width] / total).astype(jnp.bfloat16)
        for j in range(heads):
            o_ref[rows_at, j * width : (j + 1) * width] = out[j * CHUNK : (j + 1) * CHUNK]
        top[chunk] = top[chunk] + jnp.log2(total)
        product = do_rows[chunk].astype(jnp.float32) * out.astype(jnp.float32)
        coarse = product.astype(jnp.bfloat16)
        fine = (product - coarse.astype(jnp.float32)).astype(jnp.bfloat16)
        delta[chunk] = dot(coarse, ones) + dot(fine, ones)

        def back_step(i, carry):
            refs = (
                q_cols, do_rows, do_cols, keys, values, scores, top, delta, dq_acc, d_blocks
            )
            back_tile(i, i, chunk, width, refs)
            return carry

        lax.fori_loop(low, cut, back_step, 0)
        return carry

    lax.fori_loop(0, tok // CHUNK, chunk_step, 0)
    for k in range(ranks):
        at = pl.ds(pl.multiple_of((rank ^ k) * part_rows, part_rows), part_rows)
        out_parts[k][...] = o_ref[at, :]
    for k in range(2, back + 1):
        pair = jnp.maximum(last - k, 0)
        mine, other = 2 * pair + parity, 2 * pair + 1 - parity
        mine_ref, other_ref = (ref.at[k - 2] for ref in d_refs)
        put(d_blocks, mine, other, mine_ref, other_ref, width, scale)


def attend(doc_ends, prepared, own, near, arrived, far, ranks, whole):
    chunks, rows, width = prepared[0].shape
    tok = chunks * CHUNK
    heads = rows // CHUNK
    back = len(arrived)
    tiles = 2 * (back + 1)
    span = tiles * tok
    vmem = pl.BlockSpec(memory_space=pltpu.VMEM)
    smem = pl.BlockSpec(memory_space=pltpu.SMEM)
    out_part = jax.ShapeDtypeStruct((tok // ranks, heads * width), jnp.bfloat16)
    row_state = jax.ShapeDtypeStruct((chunks, rows, width), jnp.float32)
    outputs = pl.pallas_call(
        functools.partial(
            attention_kernel,
            back=back,
            whole=whole,
            ranks=ranks,
            heads=heads,
            width=width,
            scale=1.0 / math.sqrt(width),
        ),
        out_shape=[out_part] * ranks
        + [
            jax.ShapeDtypeStruct((chunks,), jnp.int32),
            jax.ShapeDtypeStruct((chunks, tiles, rows, TILE), jnp.float32),
            row_state,
            row_state,
            jax.ShapeDtypeStruct((span, width), jnp.bfloat16),
            jax.ShapeDtypeStruct((span, 2 * width), jnp.bfloat16),
            row_state,
        ]
        + [
            jax.ShapeDtypeStruct((back - 1, 2 * width, tok), dtype)
            for dtype in (jnp.float32, jnp.bfloat16)
        ],
        in_specs=[smem] + [vmem] * (6 + 2 * back),
        out_specs=[vmem] * ranks + [smem] + [vmem] * 8,
        scratch_shapes=[
            pltpu.VMEM((tok, heads * width), jnp.bfloat16),
            pltpu.VMEM((rows, 2 * width), jnp.float32),
            pltpu.VMEM((tiles, 2 * width, tok), jnp.float32),
        ],
        compiler_params=pltpu.CompilerParams(vmem_limit_bytes=KERNEL_VMEM),
        cost_estimate=pl.CostEstimate(
            flops=14 * tok * heads * width * span,
            bytes_accessed=4 * tok * heads * width * 2 + 4 * span * width * 2,
            transcendentals=tok * heads * span,
        ),
        name="attention",
    )(doc_ends, *prepared, own, near, *arrived, *far)
    return outputs[:ranks], outputs[ranks : ranks + 7], outputs[ranks + 7 :]


def near_kernel(
    q_cols,
    do_rows,
    do_cols,
    lows_ref,
    scores,
    top,
    delta,
    keys,
    values,
    dq_before,
    dq_acc,
    mine_ref,
    other_ref,
    d_blocks,
    *,
    distance,
    back,
    whole,
    width,
    scale,
):
    tok = mine_ref.shape[2]
    parity, last, _, own = here(tok, back, whole)
    first = 2 * (last - distance)
    d_blocks[...] = jnp.zeros_like(d_blocks)
    dq_acc[...] = dq_before[...]

    def chunk_step(chunk, carry):
        def back_step(i, carry):
            refs = (
                q_cols, do_rows, do_cols, keys, values, scores, top, delta, dq_acc, d_blocks
            )
            back_tile(i, i - first, chunk, width, refs)
            return carry

        stop = jnp.minimum(first + 2, own + 1)
        lax.fori_loop(jnp.maximum(lows_ref[chunk], first), stop, back_step, 0)
        return carry

    lax.fori_loop(0, tok // CHUNK, chunk_step, 0)
    put(d_blocks, parity, 1 - parity, mine_ref.at[0], other_ref.at[0], width, scale)


def attend_near(prepared, state, distance, back, whole):
    _, q_cols, do_rows, do_cols = prepared
    chunks, rows, width = do_rows.shape
    tok = chunks * CHUNK
    vmem = pl.BlockSpec(memory_space=pltpu.VMEM)
    smem = pl.BlockSpec(memory_space=pltpu.SMEM)
    return pl.pallas_call(
        functools.partial(
            near_kernel,
            distance=distance,
            back=back,
            whole=whole,
            width=width,
            scale=1.0 / math.sqrt(width),
        ),
        out_shape=[jax.ShapeDtypeStruct((chunks, rows, width), jnp.float32)]
        + [
            jax.ShapeDtypeStruct((1, 2 * width, tok), dtype)
            for dtype in (jnp.float32, jnp.bfloat16)
        ],
        in_specs=[vmem] * 3 + [smem] + [vmem] * 6,
        out_specs=[vmem] * 3,
        scratch_shapes=[pltpu.VMEM((2, 2 * width, tok), jnp.float32)],
        compiler_params=pltpu.CompilerParams(vmem_limit_bytes=KERNEL_VMEM),
        cost_estimate=pl.CostEstimate(
            flops=8 * chunks * rows * width * 2 * tok,
            bytes_accessed=4 * chunks * rows * width * 2,
            transcendentals=2 * chunks * rows * tok,
        ),
        name="near",
    )(q_cols, do_rows, do_cols, *state)


def split_kernel(grad_ref, *part_refs):
    size = part_refs[0].shape[1]
    for k, ref in enumerate(part_refs):
        at = pl.multiple_of((lax.axis_index("head") ^ k) * size, size)
        ref[...] = grad_ref[:, pl.ds(at, size)]


def split(grad_attended, ranks):
    rows, columns = grad_attended.shape
    vmem = pl.BlockSpec(memory_space=pltpu.VMEM)
    part = jax.ShapeDtypeStruct((rows, columns // ranks), grad_attended.dtype)
    return pl.pallas_call(
        split_kernel,
        out_shape=[part] * ranks,
        in_specs=[vmem],
        out_specs=[vmem] * ranks,
        compiler_params=pltpu.CompilerParams(vmem_limit_bytes=SMALL_VMEM),
        name="split",
    )(grad_attended)


def arrange_kernel(q_ref, rows_ref, cols_ref, wide):
    small = unit(q_ref.shape[2])
    wide[...] = q_ref[...].astype(jnp.float32)
    for chunk in range(rows_ref.shape[0]):
        for j in range(q_ref.shape[1]):
            rows_ref[chunk, j * CHUNK : (j + 1) * CHUNK, :] = wide[
                chunk * CHUNK : (chunk + 1) * CHUNK, j, :
            ].astype(jnp.bfloat16)
        cols_ref[chunk] = dot_nt(small, rows_ref[chunk]).astype(jnp.bfloat16)


def arrange_grads_kernel(*refs):
    parts, (rows_ref, cols_ref, grads) = refs[:-3], refs[-3:]
    width = rows_ref.shape[2]
    small = unit(width)
    size = parts[0].shape[0]
    for k, ref in enumerate(parts):
        at = pl.multiple_of((lax.axis_index("head") ^ k) * size, size)
        grads[pl.ds(at, size), :] = ref[...]
    for chunk in range(rows_ref.shape[0]):
        for j in range(rows_ref.shape[1] // CHUNK):
            rows_ref[chunk, j * CHUNK : (j + 1) * CHUNK, :] = grads[
                chunk * CHUNK : (chunk + 1) * CHUNK, j * width : (j + 1) * width
            ]
        cols_ref[chunk] = dot_nt(small, rows_ref[chunk]).astype(jnp.bfloat16)


def arrange(kernel, arrays, shape, scratch):
    tok, heads, width = shape
    vmem = pl.BlockSpec(memory_space=pltpu.VMEM)
    chunks, rows = tok // CHUNK, heads * CHUNK
    return pl.pallas_call(
        kernel,
        out_shape=[
            jax.ShapeDtypeStruct((chunks, rows, width), jnp.bfloat16),
            jax.ShapeDtypeStruct((chunks, width, rows), jnp.bfloat16),
        ],
        in_specs=[vmem] * len(arrays),
        out_specs=[vmem, vmem],
        scratch_shapes=[scratch],
        compiler_params=pltpu.CompilerParams(vmem_limit_bytes=SMALL_VMEM),
        name="arrange",
    )(*arrays)


def join_kernel(*refs):
    parts, (rows_ref, out_ref, dq_ref, wide) = refs[:-4], refs[-4:]
    size = parts[0].shape[1]
    for k, ref in enumerate(parts):
        at = pl.multiple_of((lax.axis_index("head") ^ k) * size, size)
        out_ref[:, pl.ds(at, size)] = ref[...]
    scale = 1.0 / math.sqrt(rows_ref.shape[2])
    for chunk in range(rows_ref.shape[0]):
        for j in range(dq_ref.shape[1]):
            wide[chunk * CHUNK : (chunk + 1) * CHUNK, j, :] = (
                rows_ref[chunk, j * CHUNK : (j + 1) * CHUNK, :] * scale
            )
    dq_ref[...] = wide[...].astype(jnp.bfloat16)


def join(parts, dq_rows, shape):
    rows, size = parts[0].shape
    vmem = pl.BlockSpec(memory_space=pltpu.VMEM)
    return pl.pallas_call(
        join_kernel,
        out_shape=(
            jax.ShapeDtypeStruct((rows, size * len(parts)), parts[0].dtype),
            jax.ShapeDtypeStruct(shape, jnp.bfloat16),
        ),
        in_specs=[vmem] * (len(parts) + 1),
        out_specs=(vmem, vmem),
        scratch_shapes=[pltpu.VMEM(shape, jnp.float32)],
        compiler_params=pltpu.CompilerParams(vmem_limit_bytes=SMALL_VMEM),
        name="join",
    )(*parts, dq_rows)


def merge_kernel(mine_ref, other_ref, *block_refs):
    for k, ref in enumerate(block_refs):
        ref[...] = (mine_ref[k] + other_ref[k].astype(jnp.float32)).astype(ref.dtype)


def merge(mine, other):
    vmem = pl.BlockSpec(memory_space=pltpu.VMEM)
    block = jax.ShapeDtypeStruct(mine.shape[1:], jnp.bfloat16)
    return pl.pallas_call(
        merge_kernel,
        out_shape=[block] * mine.shape[0],
        in_specs=[vmem, vmem],
        out_specs=[vmem] * mine.shape[0],
        compiler_params=pltpu.CompilerParams(vmem_limit_bytes=SMALL_VMEM),
        name="merge",
    )(mine, other)


def finish_kernel(own_ref, *refs):
    arrived = refs[:-2]
    dk_ref, dv_ref = refs[-2:]
    total = own_ref[...]
    for ref in arrived:
        total = total + ref[...].astype(jnp.float32)
    total = total.astype(jnp.bfloat16)
    width = dk_ref.shape[1]
    large = unit(dk_ref.shape[0])
    dk_ref[...] = dot_nt(large, total[:width]).astype(jnp.bfloat16)
    dv_ref[...] = dot_nt(large, total[width:]).astype(jnp.bfloat16)


def finish(own_part, arrived):
    both, tok = own_part.shape
    vmem = pl.BlockSpec(memory_space=pltpu.VMEM)
    shape = jax.ShapeDtypeStruct((tok, both // 2), jnp.bfloat16)
    return pl.pallas_call(
        finish_kernel,
        out_shape=(shape, shape),
        in_specs=[vmem] * (1 + len(arrived)),
        out_specs=(vmem, vmem),
        compiler_params=pltpu.CompilerParams(vmem_limit_bytes=SMALL_VMEM),
        name="finish",
    )(own_part, *arrived)


def shifted(block, by, count):
    pairs = [(i, i + by) for i in range(count) if 0 <= i + by < count]
    return lax.ppermute(block, "ctx", pairs)


def exchanged(block, axis, by):
    return lax.ppermute(block, axis, [(i, i ^ by) for i in range(lax.axis_size(axis))])


def after(value, *others):
    return lax.optimization_barrier((value, *others))


def body(queries, key_states, value_states, doc_lengths, grad_attended):
    tok, heads, width = queries.shape
    count = lax.axis_size("ctx")
    ranks = lax.axis_size("head")
    reach = min((DOC_MOST + tok - 2) // tok, count - 1)
    back = min((reach + 1) // 2, count // 2 - 1)
    whole = count == 8 and back == 3 and ranks == 4
    docs = jnp.arange(doc_lengths.shape[0])
    doc_ends = jnp.sum(jnp.where(docs[None] <= docs[:, None], doc_lengths[None], 0), axis=1)
    own = jnp.concatenate(
        [key_states.reshape(tok, width), value_states.reshape(tok, width)], axis=0
    )
    near = exchanged(own, "ctx", 1)
    if whole:
        beside = exchanged(own, "ctx", 2)
        across = exchanged(own, "ctx", 4)
    else:
        arrived = [shifted(own, 2 * k, count) for k in range(1, back + 1)]
    grads = split(grad_attended, ranks)
    grads = [part if k == 0 else exchanged(part, "head", k) for k, part in enumerate(grads)]
    if whole:
        far_beside = exchanged(beside, "ctx", 1)
        passed = exchanged(across, "ctx", 2)
        far_across = exchanged(across, "ctx", 1)
        passed, doc_ends, far_beside, near, *grads[1:] = after(
            passed, doc_ends, far_beside, near, *grads[1:]
        )
        far_passed = exchanged(passed, "ctx", 1)
        arrived = [beside, across, passed]
        far = [far_beside, far_across, far_passed]
    else:
        far = [exchanged(block, "ctx", 1) for block in arrived]
    prepared = arrange(
        arrange_kernel, [queries], queries.shape, pltpu.VMEM(queries.shape, jnp.float32)
    )
    prepared += arrange(
        arrange_grads_kernel,
        grads,
        queries.shape,
        pltpu.VMEM((tok, heads * width), jnp.bfloat16),
    )
    outs, state, parts = attend(doc_ends, prepared, own, near, arrived, far, ranks, whole)
    outs, (mine_far, other_far) = list(outs), parts
    dq_rows, mine1, other1 = attend_near(prepared, state, 1, back, whole)
    other_far = exchanged(other_far, "ctx", 1)
    outs[1:2] = [exchanged(part, "head", 1) for part in outs[1:2]]
    other1 = exchanged(other1, "ctx", 1)
    outs[2:] = [exchanged(part, "head", k + 2) for k, part in enumerate(outs[2:])]
    other_far, mine1, *outs[1:2] = after(other_far, mine1, *outs[1:2])
    blocks = list(merge(mine_far, other_far))
    returned = [shifted(block, -2 * (k + 2), count) for k, block in enumerate(blocks)]
    dq_rows, returned[-1] = after(dq_rows, returned[-1])
    dq_rows, mine0, other0 = attend_near(prepared, [*state[:-1], dq_rows], 0, back, whole)
    (block,) = merge(mine1, other1)
    returned.append(shifted(block, -2, count))
    other0 = exchanged(other0, "ctx", 1)
    grad_keys, grad_values = finish(mine0[0], returned + [other0[0]])
    attended, grad_queries = join(outs, dq_rows, queries.shape)
    grad_keys = grad_keys.reshape(tok, 1, width)
    grad_values = grad_values.reshape(tok, 1, width)
    return attended, grad_queries, grad_keys, grad_values


def solution(mesh):
    in_specs = (
        P("ctx", "head", None),
        P("ctx", "head", None),
        P("ctx", "head", None),
        P(),
        P(("ctx", "head"), None),
    )
    out_specs = (
        P(("ctx", "head"), None),
        P("ctx", "head", None),
        P("ctx", "head", None),
        P("ctx", "head", None),
    )
    return jax.shard_map(body, mesh=mesh, in_specs=in_specs, out_specs=out_specs, check_vma=False)
```

profile of v0, /device:TPU:0, one launch (start us, length us, event | category | flops | bytes accessed | tf_op | source)
XLA Modules:
  0.0 64.7 jit_solution(10341599866311210851)
XLA Ops:
  0.6 0.9 %pad_maximum_fusion.own_ref = bf16[512,128]{1,0:T(8,128)(2,1)S(1)} fusion(bf16[256,128]{1,0:T(8,128)(2,1)} %bitcast.8, bf16[256,128]{1,0:T(8,128)(2,1)} %bitcast.9), kind=kLoop, calls=%fused_computation | loop fusion | flops 262144 | bytes 262144 | tf_op jit(solution)/shard_map/concatenate | solution.py:481
  1.5 3.0 %collective-permute-start.4 = (bf16[512,128]{1,0:T(8,128)(2,1)S(1)}, bf16[512,128]{1,0:T(8,128)(2,1)S(1)}, u32[]{:S(2)}, u32[]{:S(2)}) collective-permute-start(bf16[512,128]{1,0:T(8,128)(2,1)S(1)} %pad_maximum_fusion.own_ref), channel_id=1, source_target_pairs={{0,4},{4,0},{8,12},{12,8},{16,20},{20,16},{24,28},{28,24},{1,5},{5... | collective-permute-start | bytes 393224 | tf_op jit(solution)/shard_map/ppermute | solution.py:465
  4.5 1.6 %collective-permute-start.2 = (bf16[512,128]{1,0:T(8,128)(2,1)S(1)}, bf16[512,128]{1,0:T(8,128)(2,1)S(1)}, u32[]{:S(2)}, u32[]{:S(2)}) collective-permute-start(bf16[512,128]{1,0:T(8,128)(2,1)S(1)} %pad_maximum_fusion.own_ref), channel_id=1, source_target_pairs={{0,8},{4,12},{8,0},{12,4},{16,24},{20,28},{24,16},{28,20},{1,9},{5... | collective-permute-start | bytes 393224 | tf_op jit(solution)/shard_map/ppermute | solution.py:465
  6.1 2.6 %collective-permute-start = (bf16[512,128]{1,0:T(8,128)(2,1)S(1)}, bf16[512,128]{1,0:T(8,128)(2,1)S(1)}, u32[]{:S(2)}, u32[]{:S(2)}) collective-permute-start(bf16[512,128]{1,0:T(8,128)(2,1)S(1)} %pad_maximum_fusion.own_ref), channel_id=1, source_target_pairs={{0,16},{4,20},{8,24},{12,28},{16,0},{20,4},{24,8},{28,12},{1,17},{... | collective-permute-start | bytes 393224 | tf_op jit(solution)/shard_map/ppermute | solution.py:465
  8.7 0.0 copy-start
  8.7 1.0 %copy-done = bf16[64,4096]{1,0:T(8,128)(2,1)S(1)} copy-done((bf16[64,4096]{1,0:T(8,128)(2,1)S(1)}, bf16[64,4096]{1,0:T(8,128)(2,1)}, u32[]{:S(2)}) %copy-start) | copy-done | bytes 524312
  9.8 0.1 collective-permute-start.5
  9.9 1.6 %collective-permute-start.6 = (bf16[64,1024]{1,0:T(8,128)(2,1)S(1)}, bf16[64,1024]{1,0:T(8,128)(2,1)S(1)}, u32[]{:S(2)}, u32[]{:S(2)}) collective-permute-start(bf16[64,1024]{1,0:T(8,128)(2,1)S(1)} %get-tuple-element.50), channel_id=1, source_target_pairs={{0,2},{1,3},{2,0},{3,1},{4,6},{5,7},{6,4},{7,5},{8,10},{9,11},{10,... | collective-permute-start | bytes 393224 | tf_op jit(solution)/shard_map/ppermute | solution.py:465
  11.4 0.0 collective-permute-done.4.near_ref
  11.4 0.3 collective-permute-start.7
  11.7 0.0 collective-permute-done.2.refs_0_
  11.7 0.5 collective-permute-start.3
  12.3 2.3 %collective-permute-done.refs_1_ = bf16[512,128]{1,0:T(8,128)(2,1)S(1)} collective-permute-done((bf16[512,128]{1,0:T(8,128)(2,1)S(1)}, bf16[512,128]{1,0:T(8,128)(2,1)S(1)}, u32[]{:S(2)}, u32[]{:S(2)}) %collective-permute-start) | collective-permute-done | bytes 131104 | tf_op jit(solution)/shard_map/ppermute | solution.py:465
  14.6 0.3 collective-permute-start.1
  14.9 0.8 %select_reduce_fusion.doc_ref = s32[8]{0:T(128)S(1)} fusion(s32[8]{0:T(128)} %param.8), kind=kLoop, calls=%fused_computation.1 | loop fusion | flops 184 | bytes 64 | tf_op jit(solution)/shard_map/reduce_sum | solution.py:480
  15.7 0.0 collective-permute-done.5.refs_1_
  15.7 0.6 collective-permute-start.8
  16.3 0.0 collective-permute-done.6.refs_2_
  16.3 1.9 %collective-permute-done.7.refs_3_ = bf16[64,1024]{1,0:T(8,128)(2,1)S(1)} collective-permute-done((bf16[64,1024]{1,0:T(8,128)(2,1)S(1)}, bf16[64,1024]{1,0:T(8,128)(2,1)S(1)}, u32[]{:S(2)}, u32[]{:S(2)}) %collective-permute-start.7) | collective-permute-done | bytes 131104 | tf_op jit(solution)/shard_map/ppermute | solution.py:465
  18.1 0.0 collective-permute-done.3.refs_3_
  18.1 1.4 %collective-permute-done.1.refs_2_ = bf16[512,128]{1,0:T(8,128)(2,1)S(1)} collective-permute-done((bf16[512,128]{1,0:T(8,128)(2,1)S(1)}, bf16[512,128]{1,0:T(8,128)(2,1)S(1)}, u32[]{:S(2)}, u32[]{:S(2)}) %collective-permute-start.1) | collective-permute-done | bytes 131104 | tf_op jit(solution)/shard_map/ppermute | solution.py:465
  19.5 0.5 collective-permute-start.9
  20.0 0.0 copy-start.1
  20.0 1.0 %copy-done.1 = bf16[256,8,128]{2,1,0:T(8,128)(2,1)S(1)} copy-done((bf16[256,8,128]{2,1,0:T(8,128)(2,1)S(1)}, bf16[256,8,128]{2,1,0:T(8,128)(2,1)}, u32[]{:S(2)}) %copy-start.1) | copy-done | bytes 524312
  21.1 1.5 %arrange.2 = (bf16[2,1024,128]{2,1,0:T(8,128)(2,1)S(1)}, bf16[2,128,1024]{2,1,0:T(8,128)(2,1)S(1)}) custom-call(bf16[256,8,128]{2,1,0:T(8,128)(2,1)S(1)} %copy-done.1), custom_call_target="tpu_custom_call" | custom-call | tf_op jit(solution)/shard_map/arrange/pallas_call | solution.py:368
  22.6 0.4 arrange.3
  23.0 0.0 collective-permute-done.8.refs_4_
  23.0 1.5 %collective-permute-done.9.refs_5_ = bf16[512,128]{1,0:T(8,128)(2,1)S(1)} collective-permute-done((bf16[512,128]{1,0:T(8,128)(2,1)S(1)}, bf16[512,128]{1,0:T(8,128)(2,1)S(1)}, u32[]{:S(2)}, u32[]{:S(2)}) %collective-permute-start.9) | collective-permute-done | bytes 131104 | tf_op jit(solution)/shard_map/ppermute | solution.py:465
  24.5 4.1 %attention.1 = (bf16[64,1024]{1,0:T(8,128)(2,1)S(1)}, bf16[64,1024]{1,0:T(8,128)(2,1)S(1)}, bf16[64,1024]{1,0:T(8,128)(2,1)S(1)}, bf16[64,1024]{1,0:T(8,128)(2,1...) custom-call(s32[8]{0:T(128)S(1)} %select_reduce_fusion.doc_ref, ...), custom_call_target="tpu_custom_call" | custom-call | flops 7516192768 | bytes 4194304 | tf_op jit(solution)/shard_map/attention/pallas_call | solution.py:197
  28.6 1.9 %collective-permute-start.10 = (bf16[2,256,256]{2,1,0:T(8,128)(2,1)S(1)}, bf16[2,256,256]{2,1,0:T(8,128)(2,1)S(1)}, u32[]{:S(2)}, u32[]{:S(2)}) collective-permute-start(bf16[2,256,256]{2,1,0:T(8,128)(2,1)S(1)} %get-tuple-element.65), channel_id=1, source_target_pairs={{0,4},{4,0},{8,12},{12,8},{16,20},{20,16},{24,28},{28,24},{1,5},{5... | collective-permute-start | bytes 786440 | tf_op jit(solution)/shard_map/ppermute | solution.py:465
  30.5 0.0 collective-permute-start.11
  30.5 0.7 %near.2 = (f32[2,1024,128]{2,1,0:T(8,128)S(1)}, f32[1,256,256]{2,1,0:T(8,128)S(1)}, bf16[1,256,256]{2,1,0:T(8,128)(2,1)S(1)}) custom-call(bf16[2,128,1024]{2,1,0:T(8,128)(2,1)S(1)} %get-tuple-element.54.q_cols, bf16[2,1024,128]{2,1,0:T(8,128)(2,1)S(1)} %get-tuple-element.59.do_rows, bf16[2,128,1024]{2,1,0:T(8,128)(2,1)S(1)} %get-tuple-element.60.do_cols, ...), custom_call_target="tpu_custom_call" | custom-call | flops 1073741824 | bytes 2097152 | tf_op jit(solution)/shard_map/near/pallas_call | solution.py:289
  31.2 0.3 collective-permute-start.16
  31.5 0.4 collective-permute-done.11.refs_1_
  31.9 4.5 %collective-permute-done.10.other_ref = bf16[2,256,256]{2,1,0:T(8,128)(2,1)S(1)} collective-permute-done((bf16[2,256,256]{2,1,0:T(8,128)(2,1)S(1)}, bf16[2,256,256]{2,1,0:T(8,128)(2,1)S(1)}, u32[]{:S(2)}, u32[]{:S(2)}) %collective-permute-start.10) | collective-permute-done | bytes 262176 | tf_op jit(solution)/shard_map/ppermute | solution.py:465
  36.4 1.3 %collective-permute-start.14 = (bf16[256,256]{1,0:T(8,128)(2,1)S(1)}, bf16[256,256]{1,0:T(8,128)(2,1)S(1)}, u32[]{:S(2)}, u32[]{:S(2)}) collective-permute-start(bf16[256,256]{1,0:T(8,128)(2,1)S(1)} %get-tuple-element.81), channel_id=1, source_target_pairs={{24,0},{28,4},{25,1},{29,5},{26,2},{30,6},{27,3},{31,7}} | collective-permute-start | bytes 393224 | tf_op jit(solution)/shard_map/ppermute | solution.py:461
  37.7 1.6 %collective-permute-start.12 = (bf16[64,1024]{1,0:T(8,128)(2,1)S(1)}, bf16[64,1024]{1,0:T(8,128)(2,1)S(1)}, u32[]{:S(2)}, u32[]{:S(2)}) collective-permute-start(bf16[64,1024]{1,0:T(8,128)(2,1)S(1)} %get-tuple-element.76), channel_id=1, source_target_pairs={{0,2},{1,3},{2,0},{3,1},{4,6},{5,7},{6,4},{7,5},{8,10},{9,11},{10,... | collective-permute-start | bytes 393224 | tf_op jit(solution)/shard_map/ppermute | solution.py:465
  39.3 0.0 collective-permute-start.13
  39.3 1.3 %collective-permute-start.15 = (bf16[256,256]{1,0:T(8,128)(2,1)S(1)}, bf16[256,256]{1,0:T(8,128)(2,1)S(1)}, u32[]{:S(2)}, u32[]{:S(2)}) collective-permute-start(bf16[256,256]{1,0:T(8,128)(2,1)S(1)} %get-tuple-element.87), channel_id=1, source_target_pairs={{16,0},{20,4},{24,8},{28,12},{17,1},{21,5},{25,9},{29,13},{18,2},{... | collective-permute-start | bytes 393224 | tf_op jit(solution)/shard_map/ppermute | solution.py:461
  40.6 0.0 collective-permute-done.16.other_ref
  40.6 1.3 %collective-permute-start.17 = (bf16[256,256]{1,0:T(8,128)(2,1)S(1)}, bf16[256,256]{1,0:T(8,128)(2,1)S(1)}, u32[]{:S(2)}, u32[]{:S(2)}) collective-permute-start(bf16[256,256]{1,0:T(8,128)(2,1)S(1)} %merge.3), channel_id=1, source_target_pairs={{8,0},{12,4},{16,8},{20,12},{24,16},{28,20},{9,1},{13,5},{17,9},{2... | collective-permute-start | bytes 393224 | tf_op jit(solution)/shard_map/ppermute | solution.py:461
  41.9 13.6 %collective-permute-done.14.refs_1_ = bf16[256,256]{1,0:T(8,128)(2,1)S(1)} collective-permute-done((bf16[256,256]{1,0:T(8,128)(2,1)S(1)}, bf16[256,256]{1,0:T(8,128)(2,1)S(1)}, u32[]{:S(2)}, u32[]{:S(2)}) %collective-permute-start.14) | collective-permute-done | bytes 131104 | tf_op jit(solution)/shard_map/ppermute | solution.py:461
  55.5 2.1 %near.3 = (f32[2,1024,128]{2,1,0:T(8,128)S(1)}, f32[1,256,256]{2,1,0:T(8,128)S(1)}, bf16[1,256,256]{2,1,0:T(8,128)(2,1)S(1)}) custom-call(bf16[2,128,1024]{2,1,0:T(8,128)(2,1)S(1)} %get-tuple-element.54.q_cols, bf16[2,1024,128]{2,1,0:T(8,128)(2,1)S(1)} %get-tuple-element.59.do_rows, bf16[2,128,1024]{2,1,0:T(8,128)(2,1)S(1)} %get-tuple-element.60.do_cols, ...), custom_call_target="tpu_custom_call" | custom-call | flops 1073741824 | bytes 2097152 | tf_op jit(solution)/shard_map/near/pallas_call | solution.py:289
  57.7 3.2 %collective-permute-start.18 = (bf16[1,256,256]{2,1,0:T(8,128)(2,1)S(1)}, bf16[1,256,256]{2,1,0:T(8,128)(2,1)S(1)}, u32[]{:S(2)}, u32[]{:S(2)}) collective-permute-start(bf16[1,256,256]{2,1,0:T(8,128)(2,1)S(1)} %get-tuple-element.91), channel_id=1, source_target_pairs={{0,4},{4,0},{8,12},{12,8},{16,20},{20,16},{24,28},{28,24},{1,5},{5... | collective-permute-start | bytes 393224 | tf_op jit(solution)/shard_map/ppermute | solution.py:465
  60.9 0.0 collective-permute-done.12.refs_2_
  60.9 0.0 collective-permute-done.13.refs_3_
  60.9 1.5 %join.1 = (bf16[64,4096]{1,0:T(8,128)(2,1)}, bf16[256,8,128]{2,1,0:T(8,128)(2,1)}) custom-call(bf16[64,1024]{1,0:T(8,128)(2,1)S(1)} %get-tuple-element.64.refs_0_, bf16[64,1024]{1,0:T(8,128)(2,1)S(1)} %collective-permute-done.11.refs_1_, bf16[64,1024]{1,0:T(8,128)(2,1)S(1)} %collective-permute-done.12.refs_2_, ...), custom_call_target="tpu_custom_call" | custom-call | tf_op jit(solution)/shard_map/join/pallas_call | solution.py:400
  62.4 0.0 collective-permute-done.15.refs_0_
  62.4 0.0 collective-permute-done.17.refs_2_
  62.4 1.4 %collective-permute-done.18 = bf16[1,256,256]{2,1,0:T(8,128)(2,1)S(1)} collective-permute-done((bf16[1,256,256]{2,1,0:T(8,128)(2,1)S(1)}, bf16[1,256,256]{2,1,0:T(8,128)(2,1)S(1)}, u32[]{:S(2)}, u32[]{:S(2)}) %collective-permute-start.18) | collective-permute-done | bytes 131104 | tf_op jit(solution)/shard_map/ppermute | solution.py:465
  63.8 0.9 %finish.1 = (bf16[256,128]{1,0:T(8,128)(2,1)}, bf16[256,128]{1,0:T(8,128)(2,1)}) custom-call(f32[256,256]{1,0:T(8,128)S(1)} %bitcast.6, bf16[256,256]{1,0:T(8,128)(2,1)S(1)} %collective-permute-done.15.refs_0_, bf16[256,256]{1,0:T(8,128)(2,1)S(1)} %collective-permute-done.14.refs_1_, bf16[256,256]{1,0:T(8,128)(2,1)S(1)} %collective-permute-done.17.refs_2_, ...), custom_call_target="tpu_custom_call" | custom-call | tf_op jit(solution)/shard_map/finish/pallas_call | solution.py:449
  (3 shorter events, 0.1 us)
Async XLA Ops:
  1.5 9.9 %collective-permute-start.4 = (bf16[512,128]{1,0:T(8,128)(2,1)S(1)}, bf16[512,128]{1,0:T(8,128)(2,1)S(1)}, u32[]{:S(2)}, u32[]{:S(2)}) collective-permute-start(bf16[512,128]{1,0:T(8,128)(2,1)S(1)} %pad_maximum_fusion.own_ref), channel_id=1, source_target_pairs={{0,4},{4,0},{8,12},{12,8},{16,20},{20,16},{24,28},{28,24},{1,5},{5... | collective-permute-start | bytes 393224 | tf_op jit(solution)/shard_map/ppermute | solution.py:465
  4.5 7.2 %collective-permute-start.2 = (bf16[512,128]{1,0:T(8,128)(2,1)S(1)}, bf16[512,128]{1,0:T(8,128)(2,1)S(1)}, u32[]{:S(2)}, u32[]{:S(2)}) collective-permute-start(bf16[512,128]{1,0:T(8,128)(2,1)S(1)} %pad_maximum_fusion.own_ref), channel_id=1, source_target_pairs={{0,8},{4,12},{8,0},{12,4},{16,24},{20,28},{24,16},{28,20},{1,9},{5... | collective-permute-start | bytes 393224 | tf_op jit(solution)/shard_map/ppermute | solution.py:465
  6.1 8.4 %collective-permute-start = (bf16[512,128]{1,0:T(8,128)(2,1)S(1)}, bf16[512,128]{1,0:T(8,128)(2,1)S(1)}, u32[]{:S(2)}, u32[]{:S(2)}) collective-permute-start(bf16[512,128]{1,0:T(8,128)(2,1)S(1)} %pad_maximum_fusion.own_ref), channel_id=1, source_target_pairs={{0,16},{4,20},{8,24},{12,28},{16,0},{20,4},{24,8},{28,12},{1,17},{... | collective-permute-start | bytes 393224 | tf_op jit(solution)/shard_map/ppermute | solution.py:465
  8.7 1.0 %copy-start = (bf16[64,4096]{1,0:T(8,128)(2,1)S(1)}, bf16[64,4096]{1,0:T(8,128)(2,1)}, u32[]{:S(2)}) copy-start(bf16[64,4096]{1,0:T(8,128)(2,1)} %grad_ref.1) | copy-start | bytes 1572868
  9.8 5.9 %collective-permute-start.5 = (bf16[64,1024]{1,0:T(8,128)(2,1)S(1)}, bf16[64,1024]{1,0:T(8,128)(2,1)S(1)}, u32[]{:S(2)}, u32[]{:S(2)}) collective-permute-start(bf16[64,1024]{1,0:T(8,128)(2,1)S(1)} %get-tuple-element.49), channel_id=1, source_target_pairs={{0,1},{1,0},{2,3},{3,2},{4,5},{5,4},{6,7},{7,6},{8,9},{9,8},{10,11... | collective-permute-start | bytes 393224 | tf_op jit(solution)/shard_map/ppermute | solution.py:465
  9.9 6.4 %collective-permute-start.6 = (bf16[64,1024]{1,0:T(8,128)(2,1)S(1)}, bf16[64,1024]{1,0:T(8,128)(2,1)S(1)}, u32[]{:S(2)}, u32[]{:S(2)}) collective-permute-start(bf16[64,1024]{1,0:T(8,128)(2,1)S(1)} %get-tuple-element.50), channel_id=1, source_target_pairs={{0,2},{1,3},{2,0},{3,1},{4,6},{5,7},{6,4},{7,5},{8,10},{9,11},{10,... | collective-permute-start | bytes 393224 | tf_op jit(solution)/shard_map/ppermute | solution.py:465
  11.4 6.7 %collective-permute-start.7 = (bf16[64,1024]{1,0:T(8,128)(2,1)S(1)}, bf16[64,1024]{1,0:T(8,128)(2,1)S(1)}, u32[]{:S(2)}, u32[]{:S(2)}) collective-permute-start(bf16[64,1024]{1,0:T(8,128)(2,1)S(1)} %get-tuple-element.51), channel_id=1, source_target_pairs={{0,3},{1,2},{2,1},{3,0},{4,7},{5,6},{6,5},{7,4},{8,11},{9,10},{10,... | collective-permute-start | bytes 393224 | tf_op jit(solution)/shard_map/ppermute | solution.py:465
  11.7 6.4 %collective-permute-start.3 = (bf16[512,128]{1,0:T(8,128)(2,1)S(1)}, bf16[512,128]{1,0:T(8,128)(2,1)S(1)}, u32[]{:S(2)}, u32[]{:S(2)}) collective-permute-start(bf16[512,128]{1,0:T(8,128)(2,1)S(1)} %collective-permute-done.2.refs_0_), channel_id=1, source_target_pairs={{0,4},{4,0},{8,12},{12,8},{16,20},{20,16},{24,28},{28,24},{1,5},{5... | collective-permute-start | bytes 393224 | tf_op jit(solution)/shard_map/ppermute | solution.py:465
  14.6 5.0 %collective-permute-start.1 = (bf16[512,128]{1,0:T(8,128)(2,1)S(1)}, bf16[512,128]{1,0:T(8,128)(2,1)S(1)}, u32[]{:S(2)}, u32[]{:S(2)}) collective-permute-start(bf16[512,128]{1,0:T(8,128)(2,1)S(1)} %collective-permute-done.refs_1_), channel_id=1, source_target_pairs={{0,8},{4,12},{8,0},{12,4},{16,24},{20,28},{24,16},{28,20},{1,9},{5... | collective-permute-start | bytes 393224 | tf_op jit(solution)/shard_map/ppermute | solution.py:465
  15.7 7.3 %collective-permute-start.8 = (bf16[512,128]{1,0:T(8,128)(2,1)S(1)}, bf16[512,128]{1,0:T(8,128)(2,1)S(1)}, u32[]{:S(2)}, u32[]{:S(2)}) collective-permute-start(bf16[512,128]{1,0:T(8,128)(2,1)S(1)} %collective-permute-done.refs_1_), channel_id=1, source_target_pairs={{0,4},{4,0},{8,12},{12,8},{16,20},{20,16},{24,28},{28,24},{1,5},{5... | collective-permute-start | bytes 393224 | tf_op jit(solution)/shard_map/ppermute | solution.py:465
  19.5 5.0 %collective-permute-start.9 = (bf16[512,128]{1,0:T(8,128)(2,1)S(1)}, bf16[512,128]{1,0:T(8,128)(2,1)S(1)}, u32[]{:S(2)}, u32[]{:S(2)}) collective-permute-start(bf16[512,128]{1,0:T(8,128)(2,1)S(1)} %collective-permute-done.1.refs_2_), channel_id=1, source_target_pairs={{0,4},{4,0},{8,12},{12,8},{16,20},{20,16},{24,28},{28,24},{1,5},{5... | collective-permute-start | bytes 393224 | tf_op jit(solution)/shard_map/ppermute | solution.py:465
  20.0 1.0 %copy-start.1 = (bf16[256,8,128]{2,1,0:T(8,128)(2,1)S(1)}, bf16[256,8,128]{2,1,0:T(8,128)(2,1)}, u32[]{:S(2)}) copy-start(bf16[256,8,128]{2,1,0:T(8,128)(2,1)} %q_ref.1) | copy-start | bytes 1572868
  28.6 7.7 %collective-permute-start.10 = (bf16[2,256,256]{2,1,0:T(8,128)(2,1)S(1)}, bf16[2,256,256]{2,1,0:T(8,128)(2,1)S(1)}, u32[]{:S(2)}, u32[]{:S(2)}) collective-permute-start(bf16[2,256,256]{2,1,0:T(8,128)(2,1)S(1)} %get-tuple-element.65), channel_id=1, source_target_pairs={{0,4},{4,0},{8,12},{12,8},{16,20},{20,16},{24,28},{28,24},{1,5},{5... | collective-permute-start | bytes 786440 | tf_op jit(solution)/shard_map/ppermute | solution.py:465
  30.5 1.3 %collective-permute-start.11 = (bf16[64,1024]{1,0:T(8,128)(2,1)S(1)}, bf16[64,1024]{1,0:T(8,128)(2,1)S(1)}, u32[]{:S(2)}, u32[]{:S(2)}) collective-permute-start(bf16[64,1024]{1,0:T(8,128)(2,1)S(1)} %get-tuple-element.74), channel_id=1, source_target_pairs={{0,1},{1,0},{2,3},{3,2},{4,5},{5,4},{6,7},{7,6},{8,9},{9,8},{10,11... | collective-permute-start | bytes 393224 | tf_op jit(solution)/shard_map/ppermute | solution.py:465
  31.2 9.4 %collective-permute-start.16 = (bf16[1,256,256]{2,1,0:T(8,128)(2,1)S(1)}, bf16[1,256,256]{2,1,0:T(8,128)(2,1)S(1)}, u32[]{:S(2)}, u32[]{:S(2)}) collective-permute-start(bf16[1,256,256]{2,1,0:T(8,128)(2,1)S(1)} %get-tuple-element.90), channel_id=1, source_target_pairs={{0,4},{4,0},{8,12},{12,8},{16,20},{20,16},{24,28},{28,24},{1,5},{5... | collective-permute-start | bytes 393224 | tf_op jit(solution)/shard_map/ppermute | solution.py:465
  36.4 19.1 %collective-permute-start.14 = (bf16[256,256]{1,0:T(8,128)(2,1)S(1)}, bf16[256,256]{1,0:T(8,128)(2,1)S(1)}, u32[]{:S(2)}, u32[]{:S(2)}) collective-permute-start(bf16[256,256]{1,0:T(8,128)(2,1)S(1)} %get-tuple-element.81), channel_id=1, source_target_pairs={{24,0},{28,4},{25,1},{29,5},{26,2},{30,6},{27,3},{31,7}} | collective-permute-start | bytes 393224 | tf_op jit(solution)/shard_map/ppermute | solution.py:461
  37.7 23.2 %collective-permute-start.12 = (bf16[64,1024]{1,0:T(8,128)(2,1)S(1)}, bf16[64,1024]{1,0:T(8,128)(2,1)S(1)}, u32[]{:S(2)}, u32[]{:S(2)}) collective-permute-start(bf16[64,1024]{1,0:T(8,128)(2,1)S(1)} %get-tuple-element.76), channel_id=1, source_target_pairs={{0,2},{1,3},{2,0},{3,1},{4,6},{5,7},{6,4},{7,5},{8,10},{9,11},{10,... | collective-permute-start | bytes 393224 | tf_op jit(solution)/shard_map/ppermute | solution.py:465
  39.3 21.6 %collective-permute-start.13 = (bf16[64,1024]{1,0:T(8,128)(2,1)S(1)}, bf16[64,1024]{1,0:T(8,128)(2,1)S(1)}, u32[]{:S(2)}, u32[]{:S(2)}) collective-permute-start(bf16[64,1024]{1,0:T(8,128)(2,1)S(1)} %get-tuple-element.77), channel_id=1, source_target_pairs={{0,3},{1,2},{2,1},{3,0},{4,7},{5,6},{6,5},{7,4},{8,11},{9,10},{10,... | collective-permute-start | bytes 393224 | tf_op jit(solution)/shard_map/ppermute | solution.py:465
  39.3 23.1 %collective-permute-start.15 = (bf16[256,256]{1,0:T(8,128)(2,1)S(1)}, bf16[256,256]{1,0:T(8,128)(2,1)S(1)}, u32[]{:S(2)}, u32[]{:S(2)}) collective-permute-start(bf16[256,256]{1,0:T(8,128)(2,1)S(1)} %get-tuple-element.87), channel_id=1, source_target_pairs={{16,0},{20,4},{24,8},{28,12},{17,1},{21,5},{25,9},{29,13},{18,2},{... | collective-permute-start | bytes 393224 | tf_op jit(solution)/shard_map/ppermute | solution.py:461
  40.6 21.7 %collective-permute-start.17 = (bf16[256,256]{1,0:T(8,128)(2,1)S(1)}, bf16[256,256]{1,0:T(8,128)(2,1)S(1)}, u32[]{:S(2)}, u32[]{:S(2)}) collective-permute-start(bf16[256,256]{1,0:T(8,128)(2,1)S(1)} %merge.3), channel_id=1, source_target_pairs={{8,0},{12,4},{16,8},{20,12},{24,16},{28,20},{9,1},{13,5},{17,9},{2... | collective-permute-start | bytes 393224 | tf_op jit(solution)/shard_map/ppermute | solution.py:461
  57.7 6.2 %collective-permute-start.18 = (bf16[1,256,256]{2,1,0:T(8,128)(2,1)S(1)}, bf16[1,256,256]{2,1,0:T(8,128)(2,1)S(1)}, u32[]{:S(2)}, u32[]{:S(2)}) collective-permute-start(bf16[1,256,256]{2,1,0:T(8,128)(2,1)S(1)} %get-tuple-element.91), channel_id=1, source_target_pairs={{0,4},{4,0},{8,12},{12,8},{16,20},{20,16},{24,28},{28,24},{1,5},{5... | collective-permute-start | bytes 393224 | tf_op jit(solution)/shard_map/ppermute | solution.py:465
where the time goes:
time: 65.1 us; the launch traced here: 64.7 us
  waiting for transfers between devices  27 us (41%)
  starting transfers between devices  21.9 us (34%)
  Pallas kernels  11.4 us (18%)
  local copies, waits for them, and re-layouts  2.08 us (3%)
  other arithmetic  1.65 us (3%)
  between operations  0.75 us (1%)
    ppermute x16, starting transfers between devices, exchanged(): lax.ppermute(block, axis, [(i, i ^ by) for i in range(lax.axis_size(axis))])  18 us
    ppermute x3, waiting for transfers between devices, shifted(): return lax.ppermute(block, 'ctx', pairs)  13.6 us
    ppermute x16, waiting for transfers between devices, exchanged(): lax.ppermute(block, axis, [(i, i ^ by) for i in range(lax.axis_size(axis))])  13.4 us
    pallas_call x1, Pallas kernels, attend(): pl.pallas_call(functools.partial(attention_kernel, back=back, whole=whole...  4.13 us
    ppermute x3, starting transfers between devices, shifted(): return lax.ppermute(block, 'ctx', pairs)  3.86 us
    pallas_call x2, Pallas kernels, attend_near(): pl.pallas_call(functools.partial(near_kernel, distance=distance, back=bac...  2.83 us
    unnamed x4, local copies, waits for them, and re-layouts  2.08 us
    pallas_call x2, Pallas kernels, arrange(): pl.pallas_call(kernel, out_shape=[jax.ShapeDtypeStruct((chunks, rows, wid...  1.87 us
  transfers between devices with their start and end apart: 19, of which 8 were waited for; matrix products, arithmetic and copies ran while one was open for 1% of the time, Pallas kernels for 10%

commit v1 on v0

--- a/solution.py
+++ b/solution.py
@@ -516,11 +516,12 @@
     other_far = exchanged(other_far, "ctx", 1)
     outs[1:2] = [exchanged(part, "head", 1) for part in outs[1:2]]
     other1 = exchanged(other1, "ctx", 1)
-    outs[2:] = [exchanged(part, "head", k + 2) for k, part in enumerate(outs[2:])]
     other_far, mine1, *outs[1:2] = after(other_far, mine1, *outs[1:2])
     blocks = list(merge(mine_far, other_far))
+    blocks[-1], *outs[2:] = after(blocks[-1], *outs[2:])
+    outs[2:] = [exchanged(part, "head", k + 2) for k, part in enumerate(outs[2:])]
     returned = [shifted(block, -2 * (k + 2), count) for k, block in enumerate(blocks)]
-    dq_rows, returned[-1] = after(dq_rows, returned[-1])
+    dq_rows, *outs[2:3] = after(dq_rows, *outs[2:3])
     dq_rows, mine0, other0 = attend_near(prepared, [*state[:-1], dq_rows], 0, back, whole)
     (block,) = merge(mine1, other1)
     returned.append(shifted(block, -2, count))

time: 65.1 us -> 62.6 us (0.962)
  the two profiles are of different devices: /device:TPU:0 before, /device:TPU:30 now
where the time goes in v1:
time: 62.6 us; the launch traced here: 62.3 us
  Pallas kernels  30.3 us (48%)
  waiting for transfers between devices  14 us (22%)
  starting transfers between devices  13.5 us (22%)
  local copies, waits for them, and re-layouts  2.08 us (3%)
  other arithmetic  1.65 us (3%)
  between operations  0.77 us (1%)
    pallas_call x1, Pallas kernels, attend(): pl.pallas_call(functools.partial(attention_kernel, back=back, whole=whole...  18.8 us
    ppermute x16, waiting for transfers between devices, exchanged(): lax.ppermute(block, axis, [(i, i ^ by) for i in range(lax.axis_size(axis))])  14 us
    ppermute x16, starting transfers between devices, exchanged(): lax.ppermute(block, axis, [(i, i ^ by) for i in range(lax.axis_size(axis))])  9.62 us
    pallas_call x2, Pallas kernels, attend_near(): pl.pallas_call(functools.partial(near_kernel, distance=distance, back=bac...  7.09 us
    ppermute x3, starting transfers between devices, shifted(): return lax.ppermute(block, 'ctx', pairs)  3.88 us
    unnamed x4, local copies, waits for them, and re-layouts  2.08 us
    pallas_call x2, Pallas kernels, arrange(): pl.pallas_call(kernel, out_shape=[jax.ShapeDtypeStruct((chunks, rows, wid...  1.87 us
    pallas_call x1, Pallas kernels, join(): pl.pallas_call(join_kernel, out_shape=(jax.ShapeDtypeStruct((rows, size *...  1.5 us
  transfers between devices with their start and end apart: 19, of which 9 were waited for; matrix products, arithmetic and copies ran while one was open for 1% of the time, Pallas kernels for 17%

profile of v1, /device:TPU:30, one launch (start us, length us, event | category | flops | bytes accessed | tf_op | source)
XLA Modules:
  0.0 62.3 jit_solution(16162687971034083944)
XLA Ops:
  0.6 0.9 %pad_maximum_fusion.own_ref = bf16[512,128]{1,0:T(8,128)(2,1)S(1)} fusion(bf16[256,128]{1,0:T(8,128)(2,1)} %bitcast.8, bf16[256,128]{1,0:T(8,128)(2,1)} %bitcast.9), kind=kLoop, calls=%fused_computation | loop fusion | flops 262144 | bytes 262144 | tf_op jit(solution)/shard_map/concatenate | solution.py:481
  1.5 0.6 collective-permute-start.4
  2.1 0.4 collective-permute-start.2
  2.5 0.3 collective-permute-start
  2.9 0.0 copy-start
  2.9 1.0 %copy-done = bf16[64,4096]{1,0:T(8,128)(2,1)S(1)} copy-done((bf16[64,4096]{1,0:T(8,128)(2,1)S(1)}, bf16[64,4096]{1,0:T(8,128)(2,1)}, u32[]{:S(2)}) %copy-start) | copy-done | bytes 524312
  4.0 0.1 collective-permute-start.5
  4.0 0.3 collective-permute-start.6
  4.3 2.5 %collective-permute-done.4.near_ref = bf16[512,128]{1,0:T(8,128)(2,1)S(1)} collective-permute-done((bf16[512,128]{1,0:T(8,128)(2,1)S(1)}, bf16[512,128]{1,0:T(8,128)(2,1)S(1)}, u32[]{:S(2)}, u32[]{:S(2)}) %collective-permute-start.4) | collective-permute-done | bytes 131104 | tf_op jit(solution)/shard_map/ppermute | solution.py:465
  6.8 0.0 collective-permute-start.7
  6.8 1.7 %collective-permute-done.2.refs_0_ = bf16[512,128]{1,0:T(8,128)(2,1)S(1)} collective-permute-done((bf16[512,128]{1,0:T(8,128)(2,1)S(1)}, bf16[512,128]{1,0:T(8,128)(2,1)S(1)}, u32[]{:S(2)}, u32[]{:S(2)}) %collective-permute-start.2) | collective-permute-done | bytes 131104 | tf_op jit(solution)/shard_map/ppermute | solution.py:465
  8.5 1.5 %collective-permute-start.3 = (bf16[512,128]{1,0:T(8,128)(2,1)S(1)}, bf16[512,128]{1,0:T(8,128)(2,1)S(1)}, u32[]{:S(2)}, u32[]{:S(2)}) collective-permute-start(bf16[512,128]{1,0:T(8,128)(2,1)S(1)} %collective-permute-done.2.refs_0_), channel_id=1, source_target_pairs={{0,4},{4,0},{8,12},{12,8},{16,20},{20,16},{24,28},{28,24},{1,5},{5... | collective-permute-start | bytes 393224 | tf_op jit(solution)/shard_map/ppermute | solution.py:465
  10.0 0.9 %collective-permute-done.refs_1_ = bf16[512,128]{1,0:T(8,128)(2,1)S(1)} collective-permute-done((bf16[512,128]{1,0:T(8,128)(2,1)S(1)}, bf16[512,128]{1,0:T(8,128)(2,1)S(1)}, u32[]{:S(2)}, u32[]{:S(2)}) %collective-permute-start) | collective-permute-done | bytes 131104 | tf_op jit(solution)/shard_map/ppermute | solution.py:465
  11.0 0.0 collective-permute-start.1
  11.0 0.8 %select_reduce_fusion.doc_ref = s32[8]{0:T(128)S(1)} fusion(s32[8]{0:T(128)} %param.8), kind=kLoop, calls=%fused_computation.1 | loop fusion | flops 184 | bytes 64 | tf_op jit(solution)/shard_map/reduce_sum | solution.py:480
  11.7 0.0 collective-permute-done.5.refs_1_
  11.7 1.7 %collective-permute-start.8 = (bf16[512,128]{1,0:T(8,128)(2,1)S(1)}, bf16[512,128]{1,0:T(8,128)(2,1)S(1)}, u32[]{:S(2)}, u32[]{:S(2)}) collective-permute-start(bf16[512,128]{1,0:T(8,128)(2,1)S(1)} %collective-permute-done.refs_1_), channel_id=1, source_target_pairs={{0,4},{4,0},{8,12},{12,8},{16,20},{20,16},{24,28},{28,24},{1,5},{5... | collective-permute-start | bytes 393224 | tf_op jit(solution)/shard_map/ppermute | solution.py:465
  13.4 0.0 collective-permute-done.6.refs_2_
  13.4 0.0 collective-permute-done.7.refs_3_
  13.4 1.4 %collective-permute-done.3.refs_3_ = bf16[512,128]{1,0:T(8,128)(2,1)S(1)} collective-permute-done((bf16[512,128]{1,0:T(8,128)(2,1)S(1)}, bf16[512,128]{1,0:T(8,128)(2,1)S(1)}, u32[]{:S(2)}, u32[]{:S(2)}) %collective-permute-start.3) | collective-permute-done | bytes 131104 | tf_op jit(solution)/shard_map/ppermute | solution.py:465
  14.8 1.2 %collective-permute-done.1.refs_2_ = bf16[512,128]{1,0:T(8,128)(2,1)S(1)} collective-permute-done((bf16[512,128]{1,0:T(8,128)(2,1)S(1)}, bf16[512,128]{1,0:T(8,128)(2,1)S(1)}, u32[]{:S(2)}, u32[]{:S(2)}) %collective-permute-start.1) | collective-permute-done | bytes 131104 | tf_op jit(solution)/shard_map/ppermute | solution.py:465
  15.9 1.6 %collective-permute-start.9 = (bf16[512,128]{1,0:T(8,128)(2,1)S(1)}, bf16[512,128]{1,0:T(8,128)(2,1)S(1)}, u32[]{:S(2)}, u32[]{:S(2)}) collective-permute-start(bf16[512,128]{1,0:T(8,128)(2,1)S(1)} %collective-permute-done.1.refs_2_), channel_id=1, source_target_pairs={{0,4},{4,0},{8,12},{12,8},{16,20},{20,16},{24,28},{28,24},{1,5},{5... | collective-permute-start | bytes 393224 | tf_op jit(solution)/shard_map/ppermute | solution.py:465
  17.5 0.0 copy-start.1
  17.5 1.0 %copy-done.1 = bf16[256,8,128]{2,1,0:T(8,128)(2,1)S(1)} copy-done((bf16[256,8,128]{2,1,0:T(8,128)(2,1)S(1)}, bf16[256,8,128]{2,1,0:T(8,128)(2,1)}, u32[]{:S(2)}) %copy-start.1) | copy-done | bytes 524312
  18.6 1.5 %arrange.2 = (bf16[2,1024,128]{2,1,0:T(8,128)(2,1)S(1)}, bf16[2,128,1024]{2,1,0:T(8,128)(2,1)S(1)}) custom-call(bf16[256,8,128]{2,1,0:T(8,128)(2,1)S(1)} %copy-done.1), custom_call_target="tpu_custom_call" | custom-call | tf_op jit(solution)/shard_map/arrange/pallas_call | solution.py:368
  20.1 0.4 arrange.3
  20.5 0.0 collective-permute-done.8.refs_4_
  20.5 0.4 collective-permute-done.9.refs_5_
  20.9 18.8 %attention.1 = (bf16[64,1024]{1,0:T(8,128)(2,1)S(1)}, bf16[64,1024]{1,0:T(8,128)(2,1)S(1)}, bf16[64,1024]{1,0:T(8,128)(2,1)S(1)}, bf16[64,1024]{1,0:T(8,128)(2,1...) custom-call(s32[8]{0:T(128)S(1)} %select_reduce_fusion.doc_ref, ...), custom_call_target="tpu_custom_call" | custom-call | flops 7516192768 | bytes 4194304 | tf_op jit(solution)/shard_map/attention/pallas_call | solution.py:197
  39.7 0.3 collective-permute-start.10
  39.9 0.0 collective-permute-start.11
  39.9 3.5 %near.2 = (f32[2,1024,128]{2,1,0:T(8,128)S(1)}, f32[1,256,256]{2,1,0:T(8,128)S(1)}, bf16[1,256,256]{2,1,0:T(8,128)(2,1)S(1)}) custom-call(bf16[2,128,1024]{2,1,0:T(8,128)(2,1)S(1)} %get-tuple-element.57.q_cols, bf16[2,1024,128]{2,1,0:T(8,128)(2,1)S(1)} %get-tuple-element.62.do_rows, bf16[2,128,1024]{2,1,0:T(8,128)(2,1)S(1)} %get-tuple-element.63.do_cols, ...), custom_call_target="tpu_custom_call" | custom-call | flops 1073741824 | bytes 2097152 | tf_op jit(solution)/shard_map/near/pallas_call | solution.py:289
  43.5 1.9 %collective-permute-start.16 = (bf16[1,256,256]{2,1,0:T(8,128)(2,1)S(1)}, bf16[1,256,256]{2,1,0:T(8,128)(2,1)S(1)}, u32[]{:S(2)}, u32[]{:S(2)}) collective-permute-start(bf16[1,256,256]{2,1,0:T(8,128)(2,1)S(1)} %get-tuple-element.96), channel_id=1, source_target_pairs={{0,4},{4,0},{8,12},{12,8},{16,20},{20,16},{24,28},{28,24},{1,5},{5... | collective-permute-start | bytes 393224 | tf_op jit(solution)/shard_map/ppermute | solution.py:465
  45.4 0.0 collective-permute-done.11.refs_1_
  45.4 0.7 %collective-permute-done.10.other_ref = bf16[2,256,256]{2,1,0:T(8,128)(2,1)S(1)} collective-permute-done((bf16[2,256,256]{2,1,0:T(8,128)(2,1)S(1)}, bf16[2,256,256]{2,1,0:T(8,128)(2,1)S(1)}, u32[]{:S(2)}, u32[]{:S(2)}) %collective-permute-start.10) | collective-permute-done | bytes 262176 | tf_op jit(solution)/shard_map/ppermute | solution.py:465
  46.2 0.6 collective-permute-start.12
  46.7 0.4 collective-permute-start.13
  47.1 1.3 %collective-permute-start.15 = (bf16[256,256]{1,0:T(8,128)(2,1)S(1)}, bf16[256,256]{1,0:T(8,128)(2,1)S(1)}, u32[]{:S(2)}, u32[]{:S(2)}) collective-permute-start(bf16[256,256]{1,0:T(8,128)(2,1)S(1)} %get-tuple-element.94), channel_id=1, source_target_pairs={{24,0},{28,4},{25,1},{29,5},{26,2},{30,6},{27,3},{31,7}} | collective-permute-start | bytes 393224 | tf_op jit(solution)/shard_map/ppermute | solution.py:461
  48.4 1.3 %collective-permute-start.14 = (bf16[256,256]{1,0:T(8,128)(2,1)S(1)}, bf16[256,256]{1,0:T(8,128)(2,1)S(1)}, u32[]{:S(2)}, u32[]{:S(2)}) collective-permute-start(bf16[256,256]{1,0:T(8,128)(2,1)S(1)} %get-tuple-element.93), channel_id=1, source_target_pairs={{16,0},{20,4},{24,8},{28,12},{17,1},{21,5},{25,9},{29,13},{18,2},{... | collective-permute-start | bytes 393224 | tf_op jit(solution)/shard_map/ppermute | solution.py:461
  49.7 0.0 collective-permute-done.16.other_ref
  49.7 1.3 %collective-permute-start.17 = (bf16[256,256]{1,0:T(8,128)(2,1)S(1)}, bf16[256,256]{1,0:T(8,128)(2,1)S(1)}, u32[]{:S(2)}, u32[]{:S(2)}) collective-permute-start(bf16[256,256]{1,0:T(8,128)(2,1)S(1)} %merge.3), channel_id=1, source_target_pairs={{8,0},{12,4},{16,8},{20,12},{24,16},{28,20},{9,1},{13,5},{17,9},{2... | collective-permute-start | bytes 393224 | tf_op jit(solution)/shard_map/ppermute | solution.py:461
  51.0 1.5 %collective-permute-done.12.refs_2_ = bf16[64,1024]{1,0:T(8,128)(2,1)S(1)} collective-permute-done((bf16[64,1024]{1,0:T(8,128)(2,1)S(1)}, bf16[64,1024]{1,0:T(8,128)(2,1)S(1)}, u32[]{:S(2)}, u32[]{:S(2)}) %collective-permute-start.12) | collective-permute-done | bytes 131104 | tf_op jit(solution)/shard_map/ppermute | solution.py:465
  52.6 3.5 %near.3 = (f32[2,1024,128]{2,1,0:T(8,128)S(1)}, f32[1,256,256]{2,1,0:T(8,128)S(1)}, bf16[1,256,256]{2,1,0:T(8,128)(2,1)S(1)}) custom-call(bf16[2,128,1024]{2,1,0:T(8,128)(2,1)S(1)} %get-tuple-element.57.q_cols, bf16[2,1024,128]{2,1,0:T(8,128)(2,1)S(1)} %get-tuple-element.62.do_rows, bf16[2,128,1024]{2,1,0:T(8,128)(2,1)S(1)} %get-tuple-element.63.do_cols, ...), custom_call_target="tpu_custom_call" | custom-call | flops 1073741824 | bytes 2097152 | tf_op jit(solution)/shard_map/near/pallas_call | solution.py:289
  56.1 0.1 collective-permute-start.18
  56.2 0.0 collective-permute-done.13.refs_3_
  56.2 1.5 %join.1 = (bf16[64,4096]{1,0:T(8,128)(2,1)}, bf16[256,8,128]{2,1,0:T(8,128)(2,1)}) custom-call(bf16[64,1024]{1,0:T(8,128)(2,1)S(1)} %get-tuple-element.67.refs_0_, bf16[64,1024]{1,0:T(8,128)(2,1)S(1)} %collective-permute-done.11.refs_1_, bf16[64,1024]{1,0:T(8,128)(2,1)S(1)} %collective-permute-done.12.refs_2_, ...), custom_call_target="tpu_custom_call" | custom-call | tf_op jit(solution)/shard_map/join/pallas_call | solution.py:400
  57.7 0.0 collective-permute-done.15.refs_1_
  57.7 0.0 collective-permute-done.14.refs_0_
  57.7 0.0 collective-permute-done.17.refs_2_
  57.7 3.7 %collective-permute-done.18 = bf16[1,256,256]{2,1,0:T(8,128)(2,1)S(1)} collective-permute-done((bf16[1,256,256]{2,1,0:T(8,128)(2,1)S(1)}, bf16[1,256,256]{2,1,0:T(8,128)(2,1)S(1)}, u32[]{:S(2)}, u32[]{:S(2)}) %collective-permute-start.18) | collective-permute-done | bytes 131104 | tf_op jit(solution)/shard_map/ppermute | solution.py:465
  61.4 0.9 %finish.1 = (bf16[256,128]{1,0:T(8,128)(2,1)}, bf16[256,128]{1,0:T(8,128)(2,1)}) custom-call(f32[256,256]{1,0:T(8,128)S(1)} %bitcast.6, bf16[256,256]{1,0:T(8,128)(2,1)S(1)} %collective-permute-done.14.refs_0_, bf16[256,256]{1,0:T(8,128)(2,1)S(1)} %collective-permute-done.15.refs_1_, bf16[256,256]{1,0:T(8,128)(2,1)S(1)} %collective-permute-done.17.refs_2_, ...), custom_call_target="tpu_custom_call" | custom-call | tf_op jit(solution)/shard_map/finish/pallas_call | solution.py:449
  (3 shorter events, 0.1 us)
Async XLA Ops:
  1.5 5.3 %collective-permute-start.4 = (bf16[512,128]{1,0:T(8,128)(2,1)S(1)}, bf16[512,128]{1,0:T(8,128)(2,1)S(1)}, u32[]{:S(2)}, u32[]{:S(2)}) collective-permute-start(bf16[512,128]{1,0:T(8,128)(2,1)S(1)} %pad_maximum_fusion.own_ref), channel_id=1, source_target_pairs={{0,4},{4,0},{8,12},{12,8},{16,20},{20,16},{24,28},{28,24},{1,5},{5... | collective-permute-start | bytes 393224 | tf_op jit(solution)/shard_map/ppermute | solution.py:465
  2.1 6.4 %collective-permute-start.2 = (bf16[512,128]{1,0:T(8,128)(2,1)S(1)}, bf16[512,128]{1,0:T(8,128)(2,1)S(1)}, u32[]{:S(2)}, u32[]{:S(2)}) collective-permute-start(bf16[512,128]{1,0:T(8,128)(2,1)S(1)} %pad_maximum_fusion.own_ref), channel_id=1, source_target_pairs={{0,8},{4,12},{8,0},{12,4},{16,24},{20,28},{24,16},{28,20},{1,9},{5... | collective-permute-start | bytes 393224 | tf_op jit(solution)/shard_map/ppermute | solution.py:465
  2.5 8.4 %collective-permute-start = (bf16[512,128]{1,0:T(8,128)(2,1)S(1)}, bf16[512,128]{1,0:T(8,128)(2,1)S(1)}, u32[]{:S(2)}, u32[]{:S(2)}) collective-permute-start(bf16[512,128]{1,0:T(8,128)(2,1)S(1)} %pad_maximum_fusion.own_ref), channel_id=1, source_target_pairs={{0,16},{4,20},{8,24},{12,28},{16,0},{20,4},{24,8},{28,12},{1,17},{... | collective-permute-start | bytes 393224 | tf_op jit(solution)/shard_map/ppermute | solution.py:465
  2.9 1.0 %copy-start = (bf16[64,4096]{1,0:T(8,128)(2,1)S(1)}, bf16[64,4096]{1,0:T(8,128)(2,1)}, u32[]{:S(2)}) copy-start(bf16[64,4096]{1,0:T(8,128)(2,1)} %grad_ref.1) | copy-start | bytes 1572868
  4.0 7.8 %collective-permute-start.5 = (bf16[64,1024]{1,0:T(8,128)(2,1)S(1)}, bf16[64,1024]{1,0:T(8,128)(2,1)S(1)}, u32[]{:S(2)}, u32[]{:S(2)}) collective-permute-start(bf16[64,1024]{1,0:T(8,128)(2,1)S(1)} %get-tuple-element.52), channel_id=1, source_target_pairs={{0,1},{1,0},{2,3},{3,2},{4,5},{5,4},{6,7},{7,6},{8,9},{9,8},{10,11... | collective-permute-start | bytes 393224 | tf_op jit(solution)/shard_map/ppermute | solution.py:465
  4.0 9.4 %collective-permute-start.6 = (bf16[64,1024]{1,0:T(8,128)(2,1)S(1)}, bf16[64,1024]{1,0:T(8,128)(2,1)S(1)}, u32[]{:S(2)}, u32[]{:S(2)}) collective-permute-start(bf16[64,1024]{1,0:T(8,128)(2,1)S(1)} %get-tuple-element.53), channel_id=1, source_target_pairs={{0,2},{1,3},{2,0},{3,1},{4,6},{5,7},{6,4},{7,5},{8,10},{9,11},{10,... | collective-permute-start | bytes 393224 | tf_op jit(solution)/shard_map/ppermute | solution.py:465
  6.8 6.6 %collective-permute-start.7 = (bf16[64,1024]{1,0:T(8,128)(2,1)S(1)}, bf16[64,1024]{1,0:T(8,128)(2,1)S(1)}, u32[]{:S(2)}, u32[]{:S(2)}) collective-permute-start(bf16[64,1024]{1,0:T(8,128)(2,1)S(1)} %get-tuple-element.54), channel_id=1, source_target_pairs={{0,3},{1,2},{2,1},{3,0},{4,7},{5,6},{6,5},{7,4},{8,11},{9,10},{10,... | collective-permute-start | bytes 393224 | tf_op jit(solution)/shard_map/ppermute | solution.py:465
  8.5 6.2 %collective-permute-start.3 = (bf16[512,128]{1,0:T(8,128)(2,1)S(1)}, bf16[512,128]{1,0:T(8,128)(2,1)S(1)}, u32[]{:S(2)}, u32[]{:S(2)}) collective-permute-start(bf16[512,128]{1,0:T(8,128)(2,1)S(1)} %collective-permute-done.2.refs_0_), channel_id=1, source_target_pairs={{0,4},{4,0},{8,12},{12,8},{16,20},{20,16},{24,28},{28,24},{1,5},{5... | collective-permute-start | bytes 393224 | tf_op jit(solution)/shard_map/ppermute | solution.py:465
  11.0 5.0 %collective-permute-start.1 = (bf16[512,128]{1,0:T(8,128)(2,1)S(1)}, bf16[512,128]{1,0:T(8,128)(2,1)S(1)}, u32[]{:S(2)}, u32[]{:S(2)}) collective-permute-start(bf16[512,128]{1,0:T(8,128)(2,1)S(1)} %collective-permute-done.refs_1_), channel_id=1, source_target_pairs={{0,8},{4,12},{8,0},{12,4},{16,24},{20,28},{24,16},{28,20},{1,9},{5... | collective-permute-start | bytes 393224 | tf_op jit(solution)/shard_map/ppermute | solution.py:465
  11.7 8.7 %collective-permute-start.8 = (bf16[512,128]{1,0:T(8,128)(2,1)S(1)}, bf16[512,128]{1,0:T(8,128)(2,1)S(1)}, u32[]{:S(2)}, u32[]{:S(2)}) collective-permute-start(bf16[512,128]{1,0:T(8,128)(2,1)S(1)} %collective-permute-done.refs_1_), channel_id=1, source_target_pairs={{0,4},{4,0},{8,12},{12,8},{16,20},{20,16},{24,28},{28,24},{1,5},{5... | collective-permute-start | bytes 393224 | tf_op jit(solution)/shard_map/ppermute | solution.py:465
  15.9 5.0 %collective-permute-start.9 = (bf16[512,128]{1,0:T(8,128)(2,1)S(1)}, bf16[512,128]{1,0:T(8,128)(2,1)S(1)}, u32[]{:S(2)}, u32[]{:S(2)}) collective-permute-start(bf16[512,128]{1,0:T(8,128)(2,1)S(1)} %collective-permute-done.1.refs_2_), channel_id=1, source_target_pairs={{0,4},{4,0},{8,12},{12,8},{16,20},{20,16},{24,28},{28,24},{1,5},{5... | collective-permute-start | bytes 393224 | tf_op jit(solution)/shard_map/ppermute | solution.py:465
  17.5 1.0 %copy-start.1 = (bf16[256,8,128]{2,1,0:T(8,128)(2,1)S(1)}, bf16[256,8,128]{2,1,0:T(8,128)(2,1)}, u32[]{:S(2)}) copy-start(bf16[256,8,128]{2,1,0:T(8,128)(2,1)} %q_ref.1) | copy-start | bytes 1572868
  39.7 6.4 %collective-permute-start.10 = (bf16[2,256,256]{2,1,0:T(8,128)(2,1)S(1)}, bf16[2,256,256]{2,1,0:T(8,128)(2,1)S(1)}, u32[]{:S(2)}, u32[]{:S(2)}) collective-permute-start(bf16[2,256,256]{2,1,0:T(8,128)(2,1)S(1)} %get-tuple-element.68), channel_id=1, source_target_pairs={{0,4},{4,0},{8,12},{12,8},{16,20},{20,16},{24,28},{28,24},{1,5},{5... | collective-permute-start | bytes 786440 | tf_op jit(solution)/shard_map/ppermute | solution.py:465
  39.9 5.5 %collective-permute-start.11 = (bf16[64,1024]{1,0:T(8,128)(2,1)S(1)}, bf16[64,1024]{1,0:T(8,128)(2,1)S(1)}, u32[]{:S(2)}, u32[]{:S(2)}) collective-permute-start(bf16[64,1024]{1,0:T(8,128)(2,1)S(1)} %get-tuple-element.77), channel_id=1, source_target_pairs={{0,1},{1,0},{2,3},{3,2},{4,5},{5,4},{6,7},{7,6},{8,9},{9,8},{10,11... | collective-permute-start | bytes 393224 | tf_op jit(solution)/shard_map/ppermute | solution.py:465
  43.5 6.2 %collective-permute-start.16 = (bf16[1,256,256]{2,1,0:T(8,128)(2,1)S(1)}, bf16[1,256,256]{2,1,0:T(8,128)(2,1)S(1)}, u32[]{:S(2)}, u32[]{:S(2)}) collective-permute-start(bf16[1,256,256]{2,1,0:T(8,128)(2,1)S(1)} %get-tuple-element.96), channel_id=1, source_target_pairs={{0,4},{4,0},{8,12},{12,8},{16,20},{20,16},{24,28},{28,24},{1,5},{5... | collective-permute-start | bytes 393224 | tf_op jit(solution)/shard_map/ppermute | solution.py:465
  46.2 6.4 %collective-permute-start.12 = (bf16[64,1024]{1,0:T(8,128)(2,1)S(1)}, bf16[64,1024]{1,0:T(8,128)(2,1)S(1)}, u32[]{:S(2)}, u32[]{:S(2)}) collective-permute-start(bf16[64,1024]{1,0:T(8,128)(2,1)S(1)} %get-tuple-element.85), channel_id=1, source_target_pairs={{0,2},{1,3},{2,0},{3,1},{4,6},{5,7},{6,4},{7,5},{8,10},{9,11},{10,... | collective-permute-start | bytes 393224 | tf_op jit(solution)/shard_map/ppermute | solution.py:465
  46.7 9.5 %collective-permute-start.13 = (bf16[64,1024]{1,0:T(8,128)(2,1)S(1)}, bf16[64,1024]{1,0:T(8,128)(2,1)S(1)}, u32[]{:S(2)}, u32[]{:S(2)}) collective-permute-start(bf16[64,1024]{1,0:T(8,128)(2,1)S(1)} %get-tuple-element.87), channel_id=1, source_target_pairs={{0,3},{1,2},{2,1},{3,0},{4,7},{5,6},{6,5},{7,4},{8,11},{9,10},{10,... | collective-permute-start | bytes 393224 | tf_op jit(solution)/shard_map/ppermute | solution.py:465
  47.1 10.6 %collective-permute-start.15 = (bf16[256,256]{1,0:T(8,128)(2,1)S(1)}, bf16[256,256]{1,0:T(8,128)(2,1)S(1)}, u32[]{:S(2)}, u32[]{:S(2)}) collective-permute-start(bf16[256,256]{1,0:T(8,128)(2,1)S(1)} %get-tuple-element.94), channel_id=1, source_target_pairs={{24,0},{28,4},{25,1},{29,5},{26,2},{30,6},{27,3},{31,7}} | collective-permute-start | bytes 393224 | tf_op jit(solution)/shard_map/ppermute | solution.py:461
  48.4 9.3 %collective-permute-start.14 = (bf16[256,256]{1,0:T(8,128)(2,1)S(1)}, bf16[256,256]{1,0:T(8,128)(2,1)S(1)}, u32[]{:S(2)}, u32[]{:S(2)}) collective-permute-start(bf16[256,256]{1,0:T(8,128)(2,1)S(1)} %get-tuple-element.93), channel_id=1, source_target_pairs={{16,0},{20,4},{24,8},{28,12},{17,1},{21,5},{25,9},{29,13},{18,2},{... | collective-permute-start | bytes 393224 | tf_op jit(solution)/shard_map/ppermute | solution.py:461
  49.7 8.0 %collective-permute-start.17 = (bf16[256,256]{1,0:T(8,128)(2,1)S(1)}, bf16[256,256]{1,0:T(8,128)(2,1)S(1)}, u32[]{:S(2)}, u32[]{:S(2)}) collective-permute-start(bf16[256,256]{1,0:T(8,128)(2,1)S(1)} %merge.3), channel_id=1, source_target_pairs={{8,0},{12,4},{16,8},{20,12},{24,16},{28,20},{9,1},{13,5},{17,9},{2... | collective-permute-start | bytes 393224 | tf_op jit(solution)/shard_map/ppermute | solution.py:461
  56.1 5.3 %collective-permute-start.18 = (bf16[1,256,256]{2,1,0:T(8,128)(2,1)S(1)}, bf16[1,256,256]{2,1,0:T(8,128)(2,1)S(1)}, u32[]{:S(2)}, u32[]{:S(2)}) collective-permute-start(bf16[1,256,256]{2,1,0:T(8,128)(2,1)S(1)} %get-tuple-element.97), channel_id=1, source_target_pairs={{0,4},{4,0},{8,12},{12,8},{16,20},{20,16},{24,28},{28,24},{1,5},{5... | collective-permute-start | bytes 393224 | tf_op jit(solution)/shard_map/ppermute | solution.py:465

commit v2 on v1

--- a/solution.py
+++ b/solution.py
@@ -487,15 +487,14 @@
         across = exchanged(own, "ctx", 4)
     else:
         arrived = [shifted(own, 2 * k, count) for k in range(1, back + 1)]
+    grad_attended, doc_ends = after(grad_attended, doc_ends)
     grads = split(grad_attended, ranks)
     grads = [part if k == 0 else exchanged(part, "head", k) for k, part in enumerate(grads)]
     if whole:
         far_beside = exchanged(beside, "ctx", 1)
         passed = exchanged(across, "ctx", 2)
         far_across = exchanged(across, "ctx", 1)
-        passed, doc_ends, far_beside, near, *grads[1:] = after(
-            passed, doc_ends, far_beside, near, *grads[1:]
-        )
+        passed, far_beside, near, *grads[1:] = after(passed, far_beside, near, *grads[1:])
         far_passed = exchanged(passed, "ctx", 1)
         arrived = [beside, across, passed]
         far = [far_beside, far_across, far_passed]

time: 62.6 us -> 62.1 us (level)
  the two profiles are of different devices: /device:TPU:30 before, /device:TPU:25 now
where the time goes in v2:
time: 62.1 us; the launch traced here: 62.2 us
  Pallas kernels  27.4 us (44%)
  starting transfers between devices  23 us (37%)
  waiting for transfers between devices  7.21 us (12%)
  local copies, waits for them, and re-layouts  2.08 us (3%)
  other arithmetic  1.65 us (3%)
  between operations  0.79 us (1%)
    ppermute x16, starting transfers between devices, exchanged(): lax.ppermute(block, axis, [(i, i ^ by) for i in range(lax.axis_size(axis))])  19.2 us
    pallas_call x1, Pallas kernels, attend(): pl.pallas_call(functools.partial(attention_kernel, back=back, whole=whole...  17.4 us
    ppermute x16, waiting for transfers between devices, exchanged(): lax.ppermute(block, axis, [(i, i ^ by) for i in range(lax.axis_size(axis))])  7.2 us
    pallas_call x2, Pallas kernels, attend_near(): pl.pallas_call(functools.partial(near_kernel, distance=distance, back=bac...  5.66 us
    ppermute x3, starting transfers between devices, shifted(): return lax.ppermute(block, 'ctx', pairs)  3.88 us
    unnamed x4, local copies, waits for them, and re-layouts  2.08 us
    pallas_call x2, Pallas kernels, arrange(): pl.pallas_call(kernel, out_shape=[jax.ShapeDtypeStruct((chunks, rows, wid...  1.88 us
    pallas_call x1, Pallas kernels, join(): pl.pallas_call(join_kernel, out_shape=(jax.ShapeDtypeStruct((rows, size *...  1.5 us
  transfers between devices with their start and end apart: 19, of which 4 were waited for; matrix products, arithmetic and copies ran while one was open for 1% of the time, Pallas kernels for 15%

profile of v2, /device:TPU:25, one launch (start us, length us, event | category | flops | bytes accessed | tf_op | source)
XLA Modules:
  0.0 62.2 jit_solution(13492103885338892539)
XLA Ops:
  0.6 0.9 %pad_maximum_fusion.own_ref = bf16[512,128]{1,0:T(8,128)(2,1)S(1)} fusion(bf16[256,128]{1,0:T(8,128)(2,1)} %bitcast.8, bf16[256,128]{1,0:T(8,128)(2,1)} %bitcast.9), kind=kLoop, calls=%fused_computation | loop fusion | flops 262144 | bytes 262144 | tf_op jit(solution)/shard_map/concatenate | solution.py:481
  1.5 1.3 %collective-permute-start.4 = (bf16[512,128]{1,0:T(8,128)(2,1)S(1)}, bf16[512,128]{1,0:T(8,128)(2,1)S(1)}, u32[]{:S(2)}, u32[]{:S(2)}) collective-permute-start(bf16[512,128]{1,0:T(8,128)(2,1)S(1)} %pad_maximum_fusion.own_ref), channel_id=1, source_target_pairs={{0,4},{4,0},{8,12},{12,8},{16,20},{20,16},{24,28},{28,24},{1,5},{5... | collective-permute-start | bytes 393224 | tf_op jit(solution)/shard_map/ppermute | solution.py:465
  2.8 0.2 collective-permute-start.2
  3.0 0.1 collective-permute-start
  3.0 0.8 %select_reduce_fusion.doc_ref = s32[8]{0:T(128)S(1)} fusion(s32[8]{0:T(128)} %param.8), kind=kLoop, calls=%fused_computation.1 | loop fusion | flops 184 | bytes 64 | tf_op jit(solution)/shard_map/reduce_sum | solution.py:480
  3.8 0.0 copy-start
  3.8 1.0 %copy-done = bf16[64,4096]{1,0:T(8,128)(2,1)S(1)} copy-done((bf16[64,4096]{1,0:T(8,128)(2,1)S(1)}, bf16[64,4096]{1,0:T(8,128)(2,1)}, u32[]{:S(2)}) %copy-start) | copy-done | bytes 524312
  4.9 1.6 %collective-permute-start.5 = (bf16[64,1024]{1,0:T(8,128)(2,1)S(1)}, bf16[64,1024]{1,0:T(8,128)(2,1)S(1)}, u32[]{:S(2)}, u32[]{:S(2)}) collective-permute-start(bf16[64,1024]{1,0:T(8,128)(2,1)S(1)} %get-tuple-element.58), channel_id=1, source_target_pairs={{0,1},{1,0},{2,3},{3,2},{4,5},{5,4},{6,7},{7,6},{8,9},{9,8},{10,11... | collective-permute-start | bytes 393224 | tf_op jit(solution)/shard_map/ppermute | solution.py:465
  6.5 1.2 %collective-permute-start.6 = (bf16[64,1024]{1,0:T(8,128)(2,1)S(1)}, bf16[64,1024]{1,0:T(8,128)(2,1)S(1)}, u32[]{:S(2)}, u32[]{:S(2)}) collective-permute-start(bf16[64,1024]{1,0:T(8,128)(2,1)S(1)} %get-tuple-element.59), channel_id=1, source_target_pairs={{0,2},{1,3},{2,0},{3,1},{4,6},{5,7},{6,4},{7,5},{8,10},{9,11},{10,... | collective-permute-start | bytes 393224 | tf_op jit(solution)/shard_map/ppermute | solution.py:465
  7.7 0.0 collective-permute-done.4.near_ref
  7.7 0.9 %collective-permute-start.7 = (bf16[64,1024]{1,0:T(8,128)(2,1)S(1)}, bf16[64,1024]{1,0:T(8,128)(2,1)S(1)}, u32[]{:S(2)}, u32[]{:S(2)}) collective-permute-start(bf16[64,1024]{1,0:T(8,128)(2,1)S(1)} %get-tuple-element.60), channel_id=1, source_target_pairs={{0,3},{1,2},{2,1},{3,0},{4,7},{5,6},{6,5},{7,4},{8,11},{9,10},{10,... | collective-permute-start | bytes 393224 | tf_op jit(solution)/shard_map/ppermute | solution.py:465
  8.6 0.0 collective-permute-done.2.refs_0_
  8.6 1.2 %collective-permute-start.3 = (bf16[512,128]{1,0:T(8,128)(2,1)S(1)}, bf16[512,128]{1,0:T(8,128)(2,1)S(1)}, u32[]{:S(2)}, u32[]{:S(2)}) collective-permute-start(bf16[512,128]{1,0:T(8,128)(2,1)S(1)} %collective-permute-done.2.refs_0_), channel_id=1, source_target_pairs={{0,4},{4,0},{8,12},{12,8},{16,20},{20,16},{24,28},{28,24},{1,5},{5... | collective-permute-start | bytes 393224 | tf_op jit(solution)/shard_map/ppermute | solution.py:465
  9.8 0.0 collective-permute-done.refs_1_
  9.8 0.2 collective-permute-start.1
  10.0 0.0 collective-permute-done.5.refs_1_
  10.0 1.0 %collective-permute-start.8 = (bf16[512,128]{1,0:T(8,128)(2,1)S(1)}, bf16[512,128]{1,0:T(8,128)(2,1)S(1)}, u32[]{:S(2)}, u32[]{:S(2)}) collective-permute-start(bf16[512,128]{1,0:T(8,128)(2,1)S(1)} %collective-permute-done.refs_1_), channel_id=1, source_target_pairs={{0,4},{4,0},{8,12},{12,8},{16,20},{20,16},{24,28},{28,24},{1,5},{5... | collective-permute-start | bytes 393224 | tf_op jit(solution)/shard_map/ppermute | solution.py:465
  11.0 0.6 collective-permute-done.6.refs_2_
  11.6 3.3 %collective-permute-done.7.refs_3_ = bf16[64,1024]{1,0:T(8,128)(2,1)S(1)} collective-permute-done((bf16[64,1024]{1,0:T(8,128)(2,1)S(1)}, bf16[64,1024]{1,0:T(8,128)(2,1)S(1)}, u32[]{:S(2)}, u32[]{:S(2)}) %collective-permute-start.7) | collective-permute-done | bytes 131104 | tf_op jit(solution)/shard_map/ppermute | solution.py:465
  14.8 0.0 collective-permute-done.3.refs_3_
  14.8 0.0 collective-permute-done.1.refs_2_
  14.8 0.0 collective-permute-start.9
  14.8 0.0 copy-start.1
  14.8 1.0 %copy-done.1 = bf16[256,8,128]{2,1,0:T(8,128)(2,1)S(1)} copy-done((bf16[256,8,128]{2,1,0:T(8,128)(2,1)S(1)}, bf16[256,8,128]{2,1,0:T(8,128)(2,1)}, u32[]{:S(2)}) %copy-start.1) | copy-done | bytes 524312
  15.9 1.5 %arrange.2 = (bf16[2,1024,128]{2,1,0:T(8,128)(2,1)S(1)}, bf16[2,128,1024]{2,1,0:T(8,128)(2,1)S(1)}) custom-call(bf16[256,8,128]{2,1,0:T(8,128)(2,1)S(1)} %copy-done.1), custom_call_target="tpu_custom_call" | custom-call | tf_op jit(solution)/shard_map/arrange/pallas_call | solution.py:368
  17.4 0.4 arrange.3
  17.8 0.0 collective-permute-done.8.refs_4_
  17.8 0.9 %collective-permute-done.9.refs_5_ = bf16[512,128]{1,0:T(8,128)(2,1)S(1)} collective-permute-done((bf16[512,128]{1,0:T(8,128)(2,1)S(1)}, bf16[512,128]{1,0:T(8,128)(2,1)S(1)}, u32[]{:S(2)}, u32[]{:S(2)}) %collective-permute-start.9) | collective-permute-done | bytes 131104 | tf_op jit(solution)/shard_map/ppermute | solution.py:465
  18.6 17.4 %attention.1 = (bf16[64,1024]{1,0:T(8,128)(2,1)S(1)}, bf16[64,1024]{1,0:T(8,128)(2,1)S(1)}, bf16[64,1024]{1,0:T(8,128)(2,1)S(1)}, bf16[64,1024]{1,0:T(8,128)(2,1...) custom-call(s32[8]{0:T(128)S(1)} %select_reduce_fusion.doc_ref, ...), custom_call_target="tpu_custom_call" | custom-call | flops 7516192768 | bytes 4194304 | tf_op jit(solution)/shard_map/attention/pallas_call | solution.py:197
  36.0 2.1 %collective-permute-start.10 = (bf16[2,256,256]{2,1,0:T(8,128)(2,1)S(1)}, bf16[2,256,256]{2,1,0:T(8,128)(2,1)S(1)}, u32[]{:S(2)}, u32[]{:S(2)}) collective-permute-start(bf16[2,256,256]{2,1,0:T(8,128)(2,1)S(1)} %get-tuple-element.70), channel_id=1, source_target_pairs={{0,4},{4,0},{8,12},{12,8},{16,20},{20,16},{24,28},{28,24},{1,5},{5... | collective-permute-start | bytes 786440 | tf_op jit(solution)/shard_map/ppermute | solution.py:465
  38.1 3.8 %collective-permute-start.11 = (bf16[64,1024]{1,0:T(8,128)(2,1)S(1)}, bf16[64,1024]{1,0:T(8,128)(2,1)S(1)}, u32[]{:S(2)}, u32[]{:S(2)}) collective-permute-start(bf16[64,1024]{1,0:T(8,128)(2,1)S(1)} %get-tuple-element.79), channel_id=1, source_target_pairs={{0,1},{1,0},{2,3},{3,2},{4,5},{5,4},{6,7},{7,6},{8,9},{9,8},{10,11... | collective-permute-start | bytes 393224 | tf_op jit(solution)/shard_map/ppermute | solution.py:465
  41.9 3.5 %near.2 = (f32[2,1024,128]{2,1,0:T(8,128)S(1)}, f32[1,256,256]{2,1,0:T(8,128)S(1)}, bf16[1,256,256]{2,1,0:T(8,128)(2,1)S(1)}) custom-call(bf16[2,128,1024]{2,1,0:T(8,128)(2,1)S(1)} %get-tuple-element.55.q_cols, bf16[2,1024,128]{2,1,0:T(8,128)(2,1)S(1)} %get-tuple-element.64.do_rows, bf16[2,128,1024]{2,1,0:T(8,128)(2,1)S(1)} %get-tuple-element.65.do_cols, ...), custom_call_target="tpu_custom_call" | custom-call | flops 1073741824 | bytes 2097152 | tf_op jit(solution)/shard_map/near/pallas_call | solution.py:289
  45.5 0.1 collective-permute-start.16
  45.5 0.0 collective-permute-done.11.refs_1_
  45.5 0.0 collective-permute-done.10.other_ref
  45.6 1.3 %collective-permute-start.12 = (bf16[64,1024]{1,0:T(8,128)(2,1)S(1)}, bf16[64,1024]{1,0:T(8,128)(2,1)S(1)}, u32[]{:S(2)}, u32[]{:S(2)}) collective-permute-start(bf16[64,1024]{1,0:T(8,128)(2,1)S(1)} %get-tuple-element.87), channel_id=1, source_target_pairs={{0,2},{1,3},{2,0},{3,1},{4,6},{5,7},{6,4},{7,5},{8,10},{9,11},{10,... | collective-permute-start | bytes 393224 | tf_op jit(solution)/shard_map/ppermute | solution.py:465
  46.9 1.2 %collective-permute-start.13 = (bf16[64,1024]{1,0:T(8,128)(2,1)S(1)}, bf16[64,1024]{1,0:T(8,128)(2,1)S(1)}, u32[]{:S(2)}, u32[]{:S(2)}) collective-permute-start(bf16[64,1024]{1,0:T(8,128)(2,1)S(1)} %get-tuple-element.89), channel_id=1, source_target_pairs={{0,3},{1,2},{2,1},{3,0},{4,7},{5,6},{6,5},{7,4},{8,11},{9,10},{10,... | collective-permute-start | bytes 393224 | tf_op jit(solution)/shard_map/ppermute | solution.py:465
  48.2 1.3 %collective-permute-start.15 = (bf16[256,256]{1,0:T(8,128)(2,1)S(1)}, bf16[256,256]{1,0:T(8,128)(2,1)S(1)}, u32[]{:S(2)}, u32[]{:S(2)}) collective-permute-start(bf16[256,256]{1,0:T(8,128)(2,1)S(1)} %get-tuple-element.96), channel_id=1, source_target_pairs={{24,0},{28,4},{25,1},{29,5},{26,2},{30,6},{27,3},{31,7}} | collective-permute-start | bytes 393224 | tf_op jit(solution)/shard_map/ppermute | solution.py:461
  49.4 1.3 %collective-permute-start.14 = (bf16[256,256]{1,0:T(8,128)(2,1)S(1)}, bf16[256,256]{1,0:T(8,128)(2,1)S(1)}, u32[]{:S(2)}, u32[]{:S(2)}) collective-permute-start(bf16[256,256]{1,0:T(8,128)(2,1)S(1)} %get-tuple-element.95), channel_id=1, source_target_pairs={{16,0},{20,4},{24,8},{28,12},{17,1},{21,5},{25,9},{29,13},{18,2},{... | collective-permute-start | bytes 393224 | tf_op jit(solution)/shard_map/ppermute | solution.py:461
  50.8 0.0 collective-permute-done.16.other_ref
  50.8 1.3 %collective-permute-start.17 = (bf16[256,256]{1,0:T(8,128)(2,1)S(1)}, bf16[256,256]{1,0:T(8,128)(2,1)S(1)}, u32[]{:S(2)}, u32[]{:S(2)}) collective-permute-start(bf16[256,256]{1,0:T(8,128)(2,1)S(1)} %merge.3), channel_id=1, source_target_pairs={{8,0},{12,4},{16,8},{20,12},{24,16},{28,20},{9,1},{13,5},{17,9},{2... | collective-permute-start | bytes 393224 | tf_op jit(solution)/shard_map/ppermute | solution.py:461
  52.1 0.0 collective-permute-done.12.refs_2_
  52.1 2.1 %near.3 = (f32[2,1024,128]{2,1,0:T(8,128)S(1)}, f32[1,256,256]{2,1,0:T(8,128)S(1)}, bf16[1,256,256]{2,1,0:T(8,128)(2,1)S(1)}) custom-call(bf16[2,128,1024]{2,1,0:T(8,128)(2,1)S(1)} %get-tuple-element.55.q_cols, bf16[2,1024,128]{2,1,0:T(8,128)(2,1)S(1)} %get-tuple-element.64.do_rows, bf16[2,128,1024]{2,1,0:T(8,128)(2,1)S(1)} %get-tuple-element.65.do_cols, ...), custom_call_target="tpu_custom_call" | custom-call | flops 1073741824 | bytes 2097152 | tf_op jit(solution)/shard_map/near/pallas_call | solution.py:289
  54.2 3.1 %collective-permute-start.18 = (bf16[1,256,256]{2,1,0:T(8,128)(2,1)S(1)}, bf16[1,256,256]{2,1,0:T(8,128)(2,1)S(1)}, u32[]{:S(2)}, u32[]{:S(2)}) collective-permute-start(bf16[1,256,256]{2,1,0:T(8,128)(2,1)S(1)} %get-tuple-element.99), channel_id=1, source_target_pairs={{0,4},{4,0},{8,12},{12,8},{16,20},{20,16},{24,28},{28,24},{1,5},{5... | collective-permute-start | bytes 393224 | tf_op jit(solution)/shard_map/ppermute | solution.py:465
  57.3 0.0 collective-permute-done.13.refs_3_
  57.3 1.5 %join.1 = (bf16[64,4096]{1,0:T(8,128)(2,1)}, bf16[256,8,128]{2,1,0:T(8,128)(2,1)}) custom-call(bf16[64,1024]{1,0:T(8,128)(2,1)S(1)} %get-tuple-element.69.refs_0_, bf16[64,1024]{1,0:T(8,128)(2,1)S(1)} %collective-permute-done.11.refs_1_, bf16[64,1024]{1,0:T(8,128)(2,1)S(1)} %collective-permute-done.12.refs_2_, ...), custom_call_target="tpu_custom_call" | custom-call | tf_op jit(solution)/shard_map/join/pallas_call | solution.py:400
  58.8 0.0 collective-permute-done.15.refs_1_
  58.8 0.0 collective-permute-done.14.refs_0_
  58.8 0.0 collective-permute-done.17.refs_2_
  58.8 2.5 %collective-permute-done.18 = bf16[1,256,256]{2,1,0:T(8,128)(2,1)S(1)} collective-permute-done((bf16[1,256,256]{2,1,0:T(8,128)(2,1)S(1)}, bf16[1,256,256]{2,1,0:T(8,128)(2,1)S(1)}, u32[]{:S(2)}, u32[]{:S(2)}) %collective-permute-start.18) | collective-permute-done | bytes 131104 | tf_op jit(solution)/shard_map/ppermute | solution.py:465
  61.3 0.9 %finish.1 = (bf16[256,128]{1,0:T(8,128)(2,1)}, bf16[256,128]{1,0:T(8,128)(2,1)}) custom-call(f32[256,256]{1,0:T(8,128)S(1)} %bitcast.6, bf16[256,256]{1,0:T(8,128)(2,1)S(1)} %collective-permute-done.14.refs_0_, bf16[256,256]{1,0:T(8,128)(2,1)S(1)} %collective-permute-done.15.refs_1_, bf16[256,256]{1,0:T(8,128)(2,1)S(1)} %collective-permute-done.17.refs_2_, ...), custom_call_target="tpu_custom_call" | custom-call | tf_op jit(solution)/shard_map/finish/pallas_call | solution.py:449
  (3 shorter events, 0.1 us)
Async XLA Ops:
  1.5 6.2 %collective-permute-start.4 = (bf16[512,128]{1,0:T(8,128)(2,1)S(1)}, bf16[512,128]{1,0:T(8,128)(2,1)S(1)}, u32[]{:S(2)}, u32[]{:S(2)}) collective-permute-start(bf16[512,128]{1,0:T(8,128)(2,1)S(1)} %pad_maximum_fusion.own_ref), channel_id=1, source_target_pairs={{0,4},{4,0},{8,12},{12,8},{16,20},{20,16},{24,28},{28,24},{1,5},{5... | collective-permute-start | bytes 393224 | tf_op jit(solution)/shard_map/ppermute | solution.py:465
  2.8 5.8 %collective-permute-start.2 = (bf16[512,128]{1,0:T(8,128)(2,1)S(1)}, bf16[512,128]{1,0:T(8,128)(2,1)S(1)}, u32[]{:S(2)}, u32[]{:S(2)}) collective-permute-start(bf16[512,128]{1,0:T(8,128)(2,1)S(1)} %pad_maximum_fusion.own_ref), channel_id=1, source_target_pairs={{0,8},{4,12},{8,0},{12,4},{16,24},{20,28},{24,16},{28,20},{1,9},{5... | collective-permute-start | bytes 393224 | tf_op jit(solution)/shard_map/ppermute | solution.py:465
  3.0 6.8 %collective-permute-start = (bf16[512,128]{1,0:T(8,128)(2,1)S(1)}, bf16[512,128]{1,0:T(8,128)(2,1)S(1)}, u32[]{:S(2)}, u32[]{:S(2)}) collective-permute-start(bf16[512,128]{1,0:T(8,128)(2,1)S(1)} %pad_maximum_fusion.own_ref), channel_id=1, source_target_pairs={{0,16},{4,20},{8,24},{12,28},{16,0},{20,4},{24,8},{28,12},{1,17},{... | collective-permute-start | bytes 393224 | tf_op jit(solution)/shard_map/ppermute | solution.py:465
  3.8 1.0 %copy-start = (bf16[64,4096]{1,0:T(8,128)(2,1)S(1)}, bf16[64,4096]{1,0:T(8,128)(2,1)}, u32[]{:S(2)}) copy-start(bf16[64,4096]{1,0:T(8,128)(2,1)} %grad_ref) | copy-start | bytes 1572868
  4.9 5.1 %collective-permute-start.5 = (bf16[64,1024]{1,0:T(8,128)(2,1)S(1)}, bf16[64,1024]{1,0:T(8,128)(2,1)S(1)}, u32[]{:S(2)}, u32[]{:S(2)}) collective-permute-start(bf16[64,1024]{1,0:T(8,128)(2,1)S(1)} %get-tuple-element.58), channel_id=1, source_target_pairs={{0,1},{1,0},{2,3},{3,2},{4,5},{5,4},{6,7},{7,6},{8,9},{9,8},{10,11... | collective-permute-start | bytes 393224 | tf_op jit(solution)/shard_map/ppermute | solution.py:465
  6.5 5.1 %collective-permute-start.6 = (bf16[64,1024]{1,0:T(8,128)(2,1)S(1)}, bf16[64,1024]{1,0:T(8,128)(2,1)S(1)}, u32[]{:S(2)}, u32[]{:S(2)}) collective-permute-start(bf16[64,1024]{1,0:T(8,128)(2,1)S(1)} %get-tuple-element.59), channel_id=1, source_target_pairs={{0,2},{1,3},{2,0},{3,1},{4,6},{5,7},{6,4},{7,5},{8,10},{9,11},{10,... | collective-permute-start | bytes 393224 | tf_op jit(solution)/shard_map/ppermute | solution.py:465
  7.7 7.1 %collective-permute-start.7 = (bf16[64,1024]{1,0:T(8,128)(2,1)S(1)}, bf16[64,1024]{1,0:T(8,128)(2,1)S(1)}, u32[]{:S(2)}, u32[]{:S(2)}) collective-permute-start(bf16[64,1024]{1,0:T(8,128)(2,1)S(1)} %get-tuple-element.60), channel_id=1, source_target_pairs={{0,3},{1,2},{2,1},{3,0},{4,7},{5,6},{6,5},{7,4},{8,11},{9,10},{10,... | collective-permute-start | bytes 393224 | tf_op jit(solution)/shard_map/ppermute | solution.py:465
  8.6 6.2 %collective-permute-start.3 = (bf16[512,128]{1,0:T(8,128)(2,1)S(1)}, bf16[512,128]{1,0:T(8,128)(2,1)S(1)}, u32[]{:S(2)}, u32[]{:S(2)}) collective-permute-start(bf16[512,128]{1,0:T(8,128)(2,1)S(1)} %collective-permute-done.2.refs_0_), channel_id=1, source_target_pairs={{0,4},{4,0},{8,12},{12,8},{16,20},{20,16},{24,28},{28,24},{1,5},{5... | collective-permute-start | bytes 393224 | tf_op jit(solution)/shard_map/ppermute | solution.py:465
  9.8 5.0 %collective-permute-start.1 = (bf16[512,128]{1,0:T(8,128)(2,1)S(1)}, bf16[512,128]{1,0:T(8,128)(2,1)S(1)}, u32[]{:S(2)}, u32[]{:S(2)}) collective-permute-start(bf16[512,128]{1,0:T(8,128)(2,1)S(1)} %collective-permute-done.refs_1_), channel_id=1, source_target_pairs={{0,8},{4,12},{8,0},{12,4},{16,24},{20,28},{24,16},{28,20},{1,9},{5... | collective-permute-start | bytes 393224 | tf_op jit(solution)/shard_map/ppermute | solution.py:465
  10.0 7.8 %collective-permute-start.8 = (bf16[512,128]{1,0:T(8,128)(2,1)S(1)}, bf16[512,128]{1,0:T(8,128)(2,1)S(1)}, u32[]{:S(2)}, u32[]{:S(2)}) collective-permute-start(bf16[512,128]{1,0:T(8,128)(2,1)S(1)} %collective-permute-done.refs_1_), channel_id=1, source_target_pairs={{0,4},{4,0},{8,12},{12,8},{16,20},{20,16},{24,28},{28,24},{1,5},{5... | collective-permute-start | bytes 393224 | tf_op jit(solution)/shard_map/ppermute | solution.py:465
  14.8 3.8 %collective-permute-start.9 = (bf16[512,128]{1,0:T(8,128)(2,1)S(1)}, bf16[512,128]{1,0:T(8,128)(2,1)S(1)}, u32[]{:S(2)}, u32[]{:S(2)}) collective-permute-start(bf16[512,128]{1,0:T(8,128)(2,1)S(1)} %collective-permute-done.1.refs_2_), channel_id=1, source_target_pairs={{0,4},{4,0},{8,12},{12,8},{16,20},{20,16},{24,28},{28,24},{1,5},{5... | collective-permute-start | bytes 393224 | tf_op jit(solution)/shard_map/ppermute | solution.py:465
  14.8 1.0 %copy-start.1 = (bf16[256,8,128]{2,1,0:T(8,128)(2,1)S(1)}, bf16[256,8,128]{2,1,0:T(8,128)(2,1)}, u32[]{:S(2)}) copy-start(bf16[256,8,128]{2,1,0:T(8,128)(2,1)} %q_ref.1) | copy-start | bytes 1572868
  36.0 9.5 %collective-permute-start.10 = (bf16[2,256,256]{2,1,0:T(8,128)(2,1)S(1)}, bf16[2,256,256]{2,1,0:T(8,128)(2,1)S(1)}, u32[]{:S(2)}, u32[]{:S(2)}) collective-permute-start(bf16[2,256,256]{2,1,0:T(8,128)(2,1)S(1)} %get-tuple-element.70), channel_id=1, source_target_pairs={{0,4},{4,0},{8,12},{12,8},{16,20},{20,16},{24,28},{28,24},{1,5},{5... | collective-permute-start | bytes 786440 | tf_op jit(solution)/shard_map/ppermute | solution.py:465
  38.1 7.4 %collective-permute-start.11 = (bf16[64,1024]{1,0:T(8,128)(2,1)S(1)}, bf16[64,1024]{1,0:T(8,128)(2,1)S(1)}, u32[]{:S(2)}, u32[]{:S(2)}) collective-permute-start(bf16[64,1024]{1,0:T(8,128)(2,1)S(1)} %get-tuple-element.79), channel_id=1, source_target_pairs={{0,1},{1,0},{2,3},{3,2},{4,5},{5,4},{6,7},{7,6},{8,9},{9,8},{10,11... | collective-permute-start | bytes 393224 | tf_op jit(solution)/shard_map/ppermute | solution.py:465
  45.5 5.3 %collective-permute-start.16 = (bf16[1,256,256]{2,1,0:T(8,128)(2,1)S(1)}, bf16[1,256,256]{2,1,0:T(8,128)(2,1)S(1)}, u32[]{:S(2)}, u32[]{:S(2)}) collective-permute-start(bf16[1,256,256]{2,1,0:T(8,128)(2,1)S(1)} %get-tuple-element.98), channel_id=1, source_target_pairs={{0,4},{4,0},{8,12},{12,8},{16,20},{20,16},{24,28},{28,24},{1,5},{5... | collective-permute-start | bytes 393224 | tf_op jit(solution)/shard_map/ppermute | solution.py:465
  45.6 6.5 %collective-permute-start.12 = (bf16[64,1024]{1,0:T(8,128)(2,1)S(1)}, bf16[64,1024]{1,0:T(8,128)(2,1)S(1)}, u32[]{:S(2)}, u32[]{:S(2)}) collective-permute-start(bf16[64,1024]{1,0:T(8,128)(2,1)S(1)} %get-tuple-element.87), channel_id=1, source_target_pairs={{0,2},{1,3},{2,0},{3,1},{4,6},{5,7},{6,4},{7,5},{8,10},{9,11},{10,... | collective-permute-start | bytes 393224 | tf_op jit(solution)/shard_map/ppermute | solution.py:465
  46.9 10.4 %collective-permute-start.13 = (bf16[64,1024]{1,0:T(8,128)(2,1)S(1)}, bf16[64,1024]{1,0:T(8,128)(2,1)S(1)}, u32[]{:S(2)}, u32[]{:S(2)}) collective-permute-start(bf16[64,1024]{1,0:T(8,128)(2,1)S(1)} %get-tuple-element.89), channel_id=1, source_target_pairs={{0,3},{1,2},{2,1},{3,0},{4,7},{5,6},{6,5},{7,4},{8,11},{9,10},{10,... | collective-permute-start | bytes 393224 | tf_op jit(solution)/shard_map/ppermute | solution.py:465
  48.2 10.7 %collective-permute-start.15 = (bf16[256,256]{1,0:T(8,128)(2,1)S(1)}, bf16[256,256]{1,0:T(8,128)(2,1)S(1)}, u32[]{:S(2)}, u32[]{:S(2)}) collective-permute-start(bf16[256,256]{1,0:T(8,128)(2,1)S(1)} %get-tuple-element.96), channel_id=1, source_target_pairs={{24,0},{28,4},{25,1},{29,5},{26,2},{30,6},{27,3},{31,7}} | collective-permute-start | bytes 393224 | tf_op jit(solution)/shard_map/ppermute | solution.py:461
  49.4 9.4 %collective-permute-start.14 = (bf16[256,256]{1,0:T(8,128)(2,1)S(1)}, bf16[256,256]{1,0:T(8,128)(2,1)S(1)}, u32[]{:S(2)}, u32[]{:S(2)}) collective-permute-start(bf16[256,256]{1,0:T(8,128)(2,1)S(1)} %get-tuple-element.95), channel_id=1, source_target_pairs={{16,0},{20,4},{24,8},{28,12},{17,1},{21,5},{25,9},{29,13},{18,2},{... | collective-permute-start | bytes 393224 | tf_op jit(solution)/shard_map/ppermute | solution.py:461
  50.8 8.0 %collective-permute-start.17 = (bf16[256,256]{1,0:T(8,128)(2,1)S(1)}, bf16[256,256]{1,0:T(8,128)(2,1)S(1)}, u32[]{:S(2)}, u32[]{:S(2)}) collective-permute-start(bf16[256,256]{1,0:T(8,128)(2,1)S(1)} %merge.3), channel_id=1, source_target_pairs={{8,0},{12,4},{16,8},{20,12},{24,16},{28,20},{9,1},{13,5},{17,9},{2... | collective-permute-start | bytes 393224 | tf_op jit(solution)/shard_map/ppermute | solution.py:461
  54.2 7.0 %collective-permute-start.18 = (bf16[1,256,256]{2,1,0:T(8,128)(2,1)S(1)}, bf16[1,256,256]{2,1,0:T(8,128)(2,1)S(1)}, u32[]{:S(2)}, u32[]{:S(2)}) collective-permute-start(bf16[1,256,256]{2,1,0:T(8,128)(2,1)S(1)} %get-tuple-element.99), channel_id=1, source_target_pairs={{0,4},{4,0},{8,12},{12,8},{16,20},{20,16},{24,28},{28,24},{1,5},{5... | collective-permute-start | bytes 393224 | tf_op jit(solution)/shard_map/ppermute | solution.py:465

commit v3 on v2

--- a/solution.py
+++ b/solution.py
@@ -487,7 +487,6 @@
         across = exchanged(own, "ctx", 4)
     else:
         arrived = [shifted(own, 2 * k, count) for k in range(1, back + 1)]
-    grad_attended, doc_ends = after(grad_attended, doc_ends)
     grads = split(grad_attended, ranks)
     grads = [part if k == 0 else exchanged(part, "head", k) for k, part in enumerate(grads)]
     if whole:
@@ -500,6 +499,8 @@
         far = [far_beside, far_across, far_passed]
     else:
         far = [exchanged(block, "ctx", 1) for block in arrived]
+    if whole:
+        queries, doc_ends, passed = after(queries, doc_ends, passed)
     prepared = arrange(
         arrange_kernel, [queries], queries.shape, pltpu.VMEM(queries.shape, jnp.float32)
     )

time: 62.1 us -> 62.3 us (level)
  the two profiles are of different devices: /device:TPU:25 before, /device:TPU:26 now
where the time goes in v3:
time: 62.3 us; the launch traced here: 62.4 us
  Pallas kernels  27.4 us (44%)
  starting transfers between devices  15.5 us (25%)
  waiting for transfers between devices  15 us (24%)
  local copies, waits for them, and re-layouts  2.08 us (3%)
  other arithmetic  1.65 us (3%)
  between operations  0.75 us (1%)
    pallas_call x1, Pallas kernels, attend(): pl.pallas_call(functools.partial(attention_kernel, back=back, whole=whole...  17.4 us
    ppermute x16, waiting for transfers between devices, exchanged(): lax.ppermute(block, axis, [(i, i ^ by) for i in range(lax.axis_size(axis))])  15 us
    ppermute x16, starting transfers between devices, exchanged(): lax.ppermute(block, axis, [(i, i ^ by) for i in range(lax.axis_size(axis))])  11.6 us
    pallas_call x2, Pallas kernels, attend_near(): pl.pallas_call(functools.partial(near_kernel, distance=distance, back=bac...  5.67 us
    ppermute x3, starting transfers between devices, shifted(): return lax.ppermute(block, 'ctx', pairs)  3.88 us
    unnamed x4, local copies, waits for them, and re-layouts  2.08 us
    pallas_call x2, Pallas kernels, arrange(): pl.pallas_call(kernel, out_shape=[jax.ShapeDtypeStruct((chunks, rows, wid...  1.87 us
    pallas_call x1, Pallas kernels, join(): pl.pallas_call(join_kernel, out_shape=(jax.ShapeDtypeStruct((rows, size *...  1.5 us
  transfers between devices with their start and end apart: 19, of which 10 were waited for; matrix products, arithmetic and copies ran while one was open for 1% of the time, Pallas kernels for 15%

profile of v3, /device:TPU:26, one launch (start us, length us, event | category | flops | bytes accessed | tf_op | source)
XLA Modules:
  0.0 62.4 jit_solution(9392979456738491398)
XLA Ops:
  0.6 0.9 %pad_maximum_fusion.own_ref = bf16[512,128]{1,0:T(8,128)(2,1)S(1)} fusion(bf16[256,128]{1,0:T(8,128)(2,1)} %bitcast.8, bf16[256,128]{1,0:T(8,128)(2,1)} %bitcast.9), kind=kLoop, calls=%fused_computation | loop fusion | flops 262144 | bytes 262144 | tf_op jit(solution)/shard_map/concatenate | solution.py:481
  1.5 1.6 %collective-permute-start.4 = (bf16[512,128]{1,0:T(8,128)(2,1)S(1)}, bf16[512,128]{1,0:T(8,128)(2,1)S(1)}, u32[]{:S(2)}, u32[]{:S(2)}) collective-permute-start(bf16[512,128]{1,0:T(8,128)(2,1)S(1)} %pad_maximum_fusion.own_ref), channel_id=1, source_target_pairs={{0,4},{4,0},{8,12},{12,8},{16,20},{20,16},{24,28},{28,24},{1,5},{5... | collective-permute-start | bytes 393224 | tf_op jit(solution)/shard_map/ppermute | solution.py:465
  3.1 0.4 collective-permute-start.2
  3.6 0.3 collective-permute-start
  3.9 0.0 copy-start
  3.9 1.0 %copy-done = bf16[64,4096]{1,0:T(8,128)(2,1)S(1)} copy-done((bf16[64,4096]{1,0:T(8,128)(2,1)S(1)}, bf16[64,4096]{1,0:T(8,128)(2,1)}, u32[]{:S(2)}) %copy-start) | copy-done | bytes 524312
  5.0 0.1 collective-permute-start.5
  5.0 0.6 collective-permute-start.6
  5.6 1.2 %collective-permute-done.4.near_ref = bf16[512,128]{1,0:T(8,128)(2,1)S(1)} collective-permute-done((bf16[512,128]{1,0:T(8,128)(2,1)S(1)}, bf16[512,128]{1,0:T(8,128)(2,1)S(1)}, u32[]{:S(2)}, u32[]{:S(2)}) %collective-permute-start.4) | collective-permute-done | bytes 131104 | tf_op jit(solution)/shard_map/ppermute | solution.py:465
  6.8 0.1 collective-permute-start.7
  6.9 2.6 %collective-permute-done.2.refs_0_ = bf16[512,128]{1,0:T(8,128)(2,1)S(1)} collective-permute-done((bf16[512,128]{1,0:T(8,128)(2,1)S(1)}, bf16[512,128]{1,0:T(8,128)(2,1)S(1)}, u32[]{:S(2)}, u32[]{:S(2)}) %collective-permute-start.2) | collective-permute-done | bytes 131104 | tf_op jit(solution)/shard_map/ppermute | solution.py:465
  9.5 0.5 collective-permute-start.3
  10.0 2.0 %collective-permute-done.refs_1_ = bf16[512,128]{1,0:T(8,128)(2,1)S(1)} collective-permute-done((bf16[512,128]{1,0:T(8,128)(2,1)S(1)}, bf16[512,128]{1,0:T(8,128)(2,1)S(1)}, u32[]{:S(2)}, u32[]{:S(2)}) %collective-permute-start) | collective-permute-done | bytes 131104 | tf_op jit(solution)/shard_map/ppermute | solution.py:465
  12.1 0.0 collective-permute-start.1
  12.1 0.0 collective-permute-done.5.refs_1_
  12.1 0.4 collective-permute-start.8
  12.5 0.0 collective-permute-done.6.refs_2_
  12.5 0.8 %collective-permute-done.7.refs_3_ = bf16[64,1024]{1,0:T(8,128)(2,1)S(1)} collective-permute-done((bf16[64,1024]{1,0:T(8,128)(2,1)S(1)}, bf16[64,1024]{1,0:T(8,128)(2,1)S(1)}, u32[]{:S(2)}, u32[]{:S(2)}) %collective-permute-start.7) | collective-permute-done | bytes 131104 | tf_op jit(solution)/shard_map/ppermute | solution.py:465
  13.3 1.9 %collective-permute-done.3.refs_3_ = bf16[512,128]{1,0:T(8,128)(2,1)S(1)} collective-permute-done((bf16[512,128]{1,0:T(8,128)(2,1)S(1)}, bf16[512,128]{1,0:T(8,128)(2,1)S(1)}, u32[]{:S(2)}, u32[]{:S(2)}) %collective-permute-start.3) | collective-permute-done | bytes 131104 | tf_op jit(solution)/shard_map/ppermute | solution.py:465
  15.2 1.8 %collective-permute-done.1.refs_2_ = bf16[512,128]{1,0:T(8,128)(2,1)S(1)} collective-permute-done((bf16[512,128]{1,0:T(8,128)(2,1)S(1)}, bf16[512,128]{1,0:T(8,128)(2,1)S(1)}, u32[]{:S(2)}, u32[]{:S(2)}) %collective-permute-start.1) | collective-permute-done | bytes 131104 | tf_op jit(solution)/shard_map/ppermute | solution.py:465
  17.0 0.4 collective-permute-start.9
  17.5 0.8 %select_reduce_fusion.doc_ref = s32[8]{0:T(128)S(1)} fusion(s32[8]{0:T(128)} %param.8), kind=kLoop, calls=%fused_computation.1 | loop fusion | flops 184 | bytes 64 | tf_op jit(solution)/shard_map/reduce_sum | solution.py:480
  18.2 0.0 copy-start.1
  18.2 1.0 %copy-done.1 = bf16[256,8,128]{2,1,0:T(8,128)(2,1)S(1)} copy-done((bf16[256,8,128]{2,1,0:T(8,128)(2,1)S(1)}, bf16[256,8,128]{2,1,0:T(8,128)(2,1)}, u32[]{:S(2)}) %copy-start.1) | copy-done | bytes 524312
  19.3 1.5 %arrange.2 = (bf16[2,1024,128]{2,1,0:T(8,128)(2,1)S(1)}, bf16[2,128,1024]{2,1,0:T(8,128)(2,1)S(1)}) custom-call(bf16[256,8,128]{2,1,0:T(8,128)(2,1)S(1)} %copy-done.1), custom_call_target="tpu_custom_call" | custom-call | tf_op jit(solution)/shard_map/arrange/pallas_call | solution.py:368
  20.8 0.4 arrange.3
  21.2 0.0 collective-permute-done.8.refs_4_
  21.2 0.8 %collective-permute-done.9.refs_5_ = bf16[512,128]{1,0:T(8,128)(2,1)S(1)} collective-permute-done((bf16[512,128]{1,0:T(8,128)(2,1)S(1)}, bf16[512,128]{1,0:T(8,128)(2,1)S(1)}, u32[]{:S(2)}, u32[]{:S(2)}) %collective-permute-start.9) | collective-permute-done | bytes 131104 | tf_op jit(solution)/shard_map/ppermute | solution.py:465
  22.0 17.4 %attention.1 = (bf16[64,1024]{1,0:T(8,128)(2,1)S(1)}, bf16[64,1024]{1,0:T(8,128)(2,1)S(1)}, bf16[64,1024]{1,0:T(8,128)(2,1)S(1)}, bf16[64,1024]{1,0:T(8,128)(2,1...) custom-call(s32[8]{0:T(128)S(1)} %select_reduce_fusion.doc_ref, ...), custom_call_target="tpu_custom_call" | custom-call | flops 7516192768 | bytes 4194304 | tf_op jit(solution)/shard_map/attention/pallas_call | solution.py:197
  39.4 2.3 %collective-permute-start.10 = (bf16[2,256,256]{2,1,0:T(8,128)(2,1)S(1)}, bf16[2,256,256]{2,1,0:T(8,128)(2,1)S(1)}, u32[]{:S(2)}, u32[]{:S(2)}) collective-permute-start(bf16[2,256,256]{2,1,0:T(8,128)(2,1)S(1)} %get-tuple-element.70), channel_id=1, source_target_pairs={{0,4},{4,0},{8,12},{12,8},{16,20},{20,16},{24,28},{28,24},{1,5},{5... | collective-permute-start | bytes 786440 | tf_op jit(solution)/shard_map/ppermute | solution.py:465
  41.6 0.0 collective-permute-start.11
  41.6 3.5 %near.2 = (f32[2,1024,128]{2,1,0:T(8,128)S(1)}, f32[1,256,256]{2,1,0:T(8,128)S(1)}, bf16[1,256,256]{2,1,0:T(8,128)(2,1)S(1)}) custom-call(bf16[2,128,1024]{2,1,0:T(8,128)(2,1)S(1)} %get-tuple-element.60.q_cols, bf16[2,1024,128]{2,1,0:T(8,128)(2,1)S(1)} %get-tuple-element.65.do_rows, bf16[2,128,1024]{2,1,0:T(8,128)(2,1)S(1)} %get-tuple-element.66.do_cols, ...), custom_call_target="tpu_custom_call" | custom-call | flops 1073741824 | bytes 2097152 | tf_op jit(solution)/shard_map/near/pallas_call | solution.py:289
  45.2 0.2 collective-permute-start.16
  45.3 0.0 collective-permute-done.11.refs_1_
  45.3 0.6 %collective-permute-done.10.other_ref = bf16[2,256,256]{2,1,0:T(8,128)(2,1)S(1)} collective-permute-done((bf16[2,256,256]{2,1,0:T(8,128)(2,1)S(1)}, bf16[2,256,256]{2,1,0:T(8,128)(2,1)S(1)}, u32[]{:S(2)}, u32[]{:S(2)}) %collective-permute-start.10) | collective-permute-done | bytes 262176 | tf_op jit(solution)/shard_map/ppermute | solution.py:465
  46.0 0.5 collective-permute-start.12
  46.5 0.7 %collective-permute-start.13 = (bf16[64,1024]{1,0:T(8,128)(2,1)S(1)}, bf16[64,1024]{1,0:T(8,128)(2,1)S(1)}, u32[]{:S(2)}, u32[]{:S(2)}) collective-permute-start(bf16[64,1024]{1,0:T(8,128)(2,1)S(1)} %get-tuple-element.89), channel_id=1, source_target_pairs={{0,3},{1,2},{2,1},{3,0},{4,7},{5,6},{6,5},{7,4},{8,11},{9,10},{10,... | collective-permute-start | bytes 393224 | tf_op jit(solution)/shard_map/ppermute | solution.py:465
  47.3 1.3 %collective-permute-start.15 = (bf16[256,256]{1,0:T(8,128)(2,1)S(1)}, bf16[256,256]{1,0:T(8,128)(2,1)S(1)}, u32[]{:S(2)}, u32[]{:S(2)}) collective-permute-start(bf16[256,256]{1,0:T(8,128)(2,1)S(1)} %get-tuple-element.96), channel_id=1, source_target_pairs={{24,0},{28,4},{25,1},{29,5},{26,2},{30,6},{27,3},{31,7}} | collective-permute-start | bytes 393224 | tf_op jit(solution)/shard_map/ppermute | solution.py:461
  48.5 1.3 %collective-permute-start.14 = (bf16[256,256]{1,0:T(8,128)(2,1)S(1)}, bf16[256,256]{1,0:T(8,128)(2,1)S(1)}, u32[]{:S(2)}, u32[]{:S(2)}) collective-permute-start(bf16[256,256]{1,0:T(8,128)(2,1)S(1)} %get-tuple-element.95), channel_id=1, source_target_pairs={{16,0},{20,4},{24,8},{28,12},{17,1},{21,5},{25,9},{29,13},{18,2},{... | collective-permute-start | bytes 393224 | tf_op jit(solution)/shard_map/ppermute | solution.py:461
  49.9 1.3 %collective-permute-done.16.other_ref = bf16[1,256,256]{2,1,0:T(8,128)(2,1)S(1)} collective-permute-done((bf16[1,256,256]{2,1,0:T(8,128)(2,1)S(1)}, bf16[1,256,256]{2,1,0:T(8,128)(2,1)S(1)}, u32[]{:S(2)}, u32[]{:S(2)}) %collective-permute-start.16) | collective-permute-done | bytes 131104 | tf_op jit(solution)/shard_map/ppermute | solution.py:465
  51.2 1.3 %collective-permute-start.17 = (bf16[256,256]{1,0:T(8,128)(2,1)S(1)}, bf16[256,256]{1,0:T(8,128)(2,1)S(1)}, u32[]{:S(2)}, u32[]{:S(2)}) collective-permute-start(bf16[256,256]{1,0:T(8,128)(2,1)S(1)} %merge.3), channel_id=1, source_target_pairs={{8,0},{12,4},{16,8},{20,12},{24,16},{28,20},{9,1},{13,5},{17,9},{2... | collective-permute-start | bytes 393224 | tf_op jit(solution)/shard_map/ppermute | solution.py:461
  52.5 0.0 collective-permute-done.12.refs_2_
  52.5 2.1 %near.3 = (f32[2,1024,128]{2,1,0:T(8,128)S(1)}, f32[1,256,256]{2,1,0:T(8,128)S(1)}, bf16[1,256,256]{2,1,0:T(8,128)(2,1)S(1)}) custom-call(bf16[2,128,1024]{2,1,0:T(8,128)(2,1)S(1)} %get-tuple-element.60.q_cols, bf16[2,1024,128]{2,1,0:T(8,128)(2,1)S(1)} %get-tuple-element.65.do_rows, bf16[2,128,1024]{2,1,0:T(8,128)(2,1)S(1)} %get-tuple-element.66.do_cols, ...), custom_call_target="tpu_custom_call" | custom-call | flops 1073741824 | bytes 2097152 | tf_op jit(solution)/shard_map/near/pallas_call | solution.py:289
  54.6 3.4 %collective-permute-start.18 = (bf16[1,256,256]{2,1,0:T(8,128)(2,1)S(1)}, bf16[1,256,256]{2,1,0:T(8,128)(2,1)S(1)}, u32[]{:S(2)}, u32[]{:S(2)}) collective-permute-start(bf16[1,256,256]{2,1,0:T(8,128)(2,1)S(1)} %get-tuple-element.99), channel_id=1, source_target_pairs={{0,4},{4,0},{8,12},{12,8},{16,20},{20,16},{24,28},{28,24},{1,5},{5... | collective-permute-start | bytes 393224 | tf_op jit(solution)/shard_map/ppermute | solution.py:465
  58.0 0.0 collective-permute-done.13.refs_3_
  58.0 1.5 %join.1 = (bf16[64,4096]{1,0:T(8,128)(2,1)}, bf16[256,8,128]{2,1,0:T(8,128)(2,1)}) custom-call(bf16[64,1024]{1,0:T(8,128)(2,1)S(1)} %get-tuple-element.69.refs_0_, bf16[64,1024]{1,0:T(8,128)(2,1)S(1)} %collective-permute-done.11.refs_1_, bf16[64,1024]{1,0:T(8,128)(2,1)S(1)} %collective-permute-done.12.refs_2_, ...), custom_call_target="tpu_custom_call" | custom-call | tf_op jit(solution)/shard_map/join/pallas_call | solution.py:400
  59.5 0.0 collective-permute-done.15.refs_1_
  59.5 0.0 collective-permute-done.14.refs_0_
  59.5 0.0 collective-permute-done.17.refs_2_
  59.6 1.9 %collective-permute-done.18 = bf16[1,256,256]{2,1,0:T(8,128)(2,1)S(1)} collective-permute-done((bf16[1,256,256]{2,1,0:T(8,128)(2,1)S(1)}, bf16[1,256,256]{2,1,0:T(8,128)(2,1)S(1)}, u32[]{:S(2)}, u32[]{:S(2)}) %collective-permute-start.18) | collective-permute-done | bytes 131104 | tf_op jit(solution)/shard_map/ppermute | solution.py:465
  61.5 0.9 %finish.1 = (bf16[256,128]{1,0:T(8,128)(2,1)}, bf16[256,128]{1,0:T(8,128)(2,1)}) custom-call(f32[256,256]{1,0:T(8,128)S(1)} %bitcast.6, bf16[256,256]{1,0:T(8,128)(2,1)S(1)} %collective-permute-done.14.refs_0_, bf16[256,256]{1,0:T(8,128)(2,1)S(1)} %collective-permute-done.15.refs_1_, bf16[256,256]{1,0:T(8,128)(2,1)S(1)} %collective-permute-done.17.refs_2_, ...), custom_call_target="tpu_custom_call" | custom-call | tf_op jit(solution)/shard_map/finish/pallas_call | solution.py:449
  (3 shorter events, 0.1 us)
Async XLA Ops:
  1.5 5.3 %collective-permute-start.4 = (bf16[512,128]{1,0:T(8,128)(2,1)S(1)}, bf16[512,128]{1,0:T(8,128)(2,1)S(1)}, u32[]{:S(2)}, u32[]{:S(2)}) collective-permute-start(bf16[512,128]{1,0:T(8,128)(2,1)S(1)} %pad_maximum_fusion.own_ref), channel_id=1, source_target_pairs={{0,4},{4,0},{8,12},{12,8},{16,20},{20,16},{24,28},{28,24},{1,5},{5... | collective-permute-start | bytes 393224 | tf_op jit(solution)/shard_map/ppermute | solution.py:465
  3.1 6.4 %collective-permute-start.2 = (bf16[512,128]{1,0:T(8,128)(2,1)S(1)}, bf16[512,128]{1,0:T(8,128)(2,1)S(1)}, u32[]{:S(2)}, u32[]{:S(2)}) collective-permute-start(bf16[512,128]{1,0:T(8,128)(2,1)S(1)} %pad_maximum_fusion.own_ref), channel_id=1, source_target_pairs={{0,8},{4,12},{8,0},{12,4},{16,24},{20,28},{24,16},{28,20},{1,9},{5... | collective-permute-start | bytes 393224 | tf_op jit(solution)/shard_map/ppermute | solution.py:465
  3.6 8.5 %collective-permute-start = (bf16[512,128]{1,0:T(8,128)(2,1)S(1)}, bf16[512,128]{1,0:T(8,128)(2,1)S(1)}, u32[]{:S(2)}, u32[]{:S(2)}) collective-permute-start(bf16[512,128]{1,0:T(8,128)(2,1)S(1)} %pad_maximum_fusion.own_ref), channel_id=1, source_target_pairs={{0,16},{4,20},{8,24},{12,28},{16,0},{20,4},{24,8},{28,12},{1,17},{... | collective-permute-start | bytes 393224 | tf_op jit(solution)/shard_map/ppermute | solution.py:465
  3.9 1.0 %copy-start = (bf16[64,4096]{1,0:T(8,128)(2,1)S(1)}, bf16[64,4096]{1,0:T(8,128)(2,1)}, u32[]{:S(2)}) copy-start(bf16[64,4096]{1,0:T(8,128)(2,1)} %grad_ref.1) | copy-start | bytes 1572868
  5.0 7.1 %collective-permute-start.5 = (bf16[64,1024]{1,0:T(8,128)(2,1)S(1)}, bf16[64,1024]{1,0:T(8,128)(2,1)S(1)}, u32[]{:S(2)}, u32[]{:S(2)}) collective-permute-start(bf16[64,1024]{1,0:T(8,128)(2,1)S(1)} %get-tuple-element.53), channel_id=1, source_target_pairs={{0,1},{1,0},{2,3},{3,2},{4,5},{5,4},{6,7},{7,6},{8,9},{9,8},{10,11... | collective-permute-start | bytes 393224 | tf_op jit(solution)/shard_map/ppermute | solution.py:465
  5.0 7.5 %collective-permute-start.6 = (bf16[64,1024]{1,0:T(8,128)(2,1)S(1)}, bf16[64,1024]{1,0:T(8,128)(2,1)S(1)}, u32[]{:S(2)}, u32[]{:S(2)}) collective-permute-start(bf16[64,1024]{1,0:T(8,128)(2,1)S(1)} %get-tuple-element.54), channel_id=1, source_target_pairs={{0,2},{1,3},{2,0},{3,1},{4,6},{5,7},{6,4},{7,5},{8,10},{9,11},{10,... | collective-permute-start | bytes 393224 | tf_op jit(solution)/shard_map/ppermute | solution.py:465
  6.8 6.5 %collective-permute-start.7 = (bf16[64,1024]{1,0:T(8,128)(2,1)S(1)}, bf16[64,1024]{1,0:T(8,128)(2,1)S(1)}, u32[]{:S(2)}, u32[]{:S(2)}) collective-permute-start(bf16[64,1024]{1,0:T(8,128)(2,1)S(1)} %get-tuple-element.55), channel_id=1, source_target_pairs={{0,3},{1,2},{2,1},{3,0},{4,7},{5,6},{6,5},{7,4},{8,11},{9,10},{10,... | collective-permute-start | bytes 393224 | tf_op jit(solution)/shard_map/ppermute | solution.py:465
  9.5 5.7 %collective-permute-start.3 = (bf16[512,128]{1,0:T(8,128)(2,1)S(1)}, bf16[512,128]{1,0:T(8,128)(2,1)S(1)}, u32[]{:S(2)}, u32[]{:S(2)}) collective-permute-start(bf16[512,128]{1,0:T(8,128)(2,1)S(1)} %collective-permute-done.2.refs_0_), channel_id=1, source_target_pairs={{0,4},{4,0},{8,12},{12,8},{16,20},{20,16},{24,28},{28,24},{1,5},{5... | collective-permute-start | bytes 393224 | tf_op jit(solution)/shard_map/ppermute | solution.py:465
  12.1 5.0 %collective-permute-start.1 = (bf16[512,128]{1,0:T(8,128)(2,1)S(1)}, bf16[512,128]{1,0:T(8,128)(2,1)S(1)}, u32[]{:S(2)}, u32[]{:S(2)}) collective-permute-start(bf16[512,128]{1,0:T(8,128)(2,1)S(1)} %collective-permute-done.refs_1_), channel_id=1, source_target_pairs={{0,8},{4,12},{8,0},{12,4},{16,24},{20,28},{24,16},{28,20},{1,9},{5... | collective-permute-start | bytes 393224 | tf_op jit(solution)/shard_map/ppermute | solution.py:465
  12.1 9.1 %collective-permute-start.8 = (bf16[512,128]{1,0:T(8,128)(2,1)S(1)}, bf16[512,128]{1,0:T(8,128)(2,1)S(1)}, u32[]{:S(2)}, u32[]{:S(2)}) collective-permute-start(bf16[512,128]{1,0:T(8,128)(2,1)S(1)} %collective-permute-done.refs_1_), channel_id=1, source_target_pairs={{0,4},{4,0},{8,12},{12,8},{16,20},{20,16},{24,28},{28,24},{1,5},{5... | collective-permute-start | bytes 393224 | tf_op jit(solution)/shard_map/ppermute | solution.py:465
  17.0 5.0 %collective-permute-start.9 = (bf16[512,128]{1,0:T(8,128)(2,1)S(1)}, bf16[512,128]{1,0:T(8,128)(2,1)S(1)}, u32[]{:S(2)}, u32[]{:S(2)}) collective-permute-start(bf16[512,128]{1,0:T(8,128)(2,1)S(1)} %collective-permute-done.1.refs_2_), channel_id=1, source_target_pairs={{0,4},{4,0},{8,12},{12,8},{16,20},{20,16},{24,28},{28,24},{1,5},{5... | collective-permute-start | bytes 393224 | tf_op jit(solution)/shard_map/ppermute | solution.py:465
  18.2 1.0 %copy-start.1 = (bf16[256,8,128]{2,1,0:T(8,128)(2,1)S(1)}, bf16[256,8,128]{2,1,0:T(8,128)(2,1)}, u32[]{:S(2)}) copy-start(bf16[256,8,128]{2,1,0:T(8,128)(2,1)} %q_ref) | copy-start | bytes 1572868
  39.4 6.6 %collective-permute-start.10 = (bf16[2,256,256]{2,1,0:T(8,128)(2,1)S(1)}, bf16[2,256,256]{2,1,0:T(8,128)(2,1)S(1)}, u32[]{:S(2)}, u32[]{:S(2)}) collective-permute-start(bf16[2,256,256]{2,1,0:T(8,128)(2,1)S(1)} %get-tuple-element.70), channel_id=1, source_target_pairs={{0,4},{4,0},{8,12},{12,8},{16,20},{20,16},{24,28},{28,24},{1,5},{5... | collective-permute-start | bytes 786440 | tf_op jit(solution)/shard_map/ppermute | solution.py:465
  41.6 3.7 %collective-permute-start.11 = (bf16[64,1024]{1,0:T(8,128)(2,1)S(1)}, bf16[64,1024]{1,0:T(8,128)(2,1)S(1)}, u32[]{:S(2)}, u32[]{:S(2)}) collective-permute-start(bf16[64,1024]{1,0:T(8,128)(2,1)S(1)} %get-tuple-element.79), channel_id=1, source_target_pairs={{0,1},{1,0},{2,3},{3,2},{4,5},{5,4},{6,7},{7,6},{8,9},{9,8},{10,11... | collective-permute-start | bytes 393224 | tf_op jit(solution)/shard_map/ppermute | solution.py:465
  45.2 6.0 %collective-permute-start.16 = (bf16[1,256,256]{2,1,0:T(8,128)(2,1)S(1)}, bf16[1,256,256]{2,1,0:T(8,128)(2,1)S(1)}, u32[]{:S(2)}, u32[]{:S(2)}) collective-permute-start(bf16[1,256,256]{2,1,0:T(8,128)(2,1)S(1)} %get-tuple-element.98), channel_id=1, source_target_pairs={{0,4},{4,0},{8,12},{12,8},{16,20},{20,16},{24,28},{28,24},{1,5},{5... | collective-permute-start | bytes 393224 | tf_op jit(solution)/shard_map/ppermute | solution.py:465
  46.0 6.5 %collective-permute-start.12 = (bf16[64,1024]{1,0:T(8,128)(2,1)S(1)}, bf16[64,1024]{1,0:T(8,128)(2,1)S(1)}, u32[]{:S(2)}, u32[]{:S(2)}) collective-permute-start(bf16[64,1024]{1,0:T(8,128)(2,1)S(1)} %get-tuple-element.87), channel_id=1, source_target_pairs={{0,2},{1,3},{2,0},{3,1},{4,6},{5,7},{6,4},{7,5},{8,10},{9,11},{10,... | collective-permute-start | bytes 393224 | tf_op jit(solution)/shard_map/ppermute | solution.py:465
  46.5 11.5 %collective-permute-start.13 = (bf16[64,1024]{1,0:T(8,128)(2,1)S(1)}, bf16[64,1024]{1,0:T(8,128)(2,1)S(1)}, u32[]{:S(2)}, u32[]{:S(2)}) collective-permute-start(bf16[64,1024]{1,0:T(8,128)(2,1)S(1)} %get-tuple-element.89), channel_id=1, source_target_pairs={{0,3},{1,2},{2,1},{3,0},{4,7},{5,6},{6,5},{7,4},{8,11},{9,10},{10,... | collective-permute-start | bytes 393224 | tf_op jit(solution)/shard_map/ppermute | solution.py:465
  47.3 12.3 %collective-permute-start.15 = (bf16[256,256]{1,0:T(8,128)(2,1)S(1)}, bf16[256,256]{1,0:T(8,128)(2,1)S(1)}, u32[]{:S(2)}, u32[]{:S(2)}) collective-permute-start(bf16[256,256]{1,0:T(8,128)(2,1)S(1)} %get-tuple-element.96), channel_id=1, source_target_pairs={{24,0},{28,4},{25,1},{29,5},{26,2},{30,6},{27,3},{31,7}} | collective-permute-start | bytes 393224 | tf_op jit(solution)/shard_map/ppermute | solution.py:461
  48.5 11.0 %collective-permute-start.14 = (bf16[256,256]{1,0:T(8,128)(2,1)S(1)}, bf16[256,256]{1,0:T(8,128)(2,1)S(1)}, u32[]{:S(2)}, u32[]{:S(2)}) collective-permute-start(bf16[256,256]{1,0:T(8,128)(2,1)S(1)} %get-tuple-element.95), channel_id=1, source_target_pairs={{16,0},{20,4},{24,8},{28,12},{17,1},{21,5},{25,9},{29,13},{18,2},{... | collective-permute-start | bytes 393224 | tf_op jit(solution)/shard_map/ppermute | solution.py:461
  51.2 8.4 %collective-permute-start.17 = (bf16[256,256]{1,0:T(8,128)(2,1)S(1)}, bf16[256,256]{1,0:T(8,128)(2,1)S(1)}, u32[]{:S(2)}, u32[]{:S(2)}) collective-permute-start(bf16[256,256]{1,0:T(8,128)(2,1)S(1)} %merge.3), channel_id=1, source_target_pairs={{8,0},{12,4},{16,8},{20,12},{24,16},{28,20},{9,1},{13,5},{17,9},{2... | collective-permute-start | bytes 393224 | tf_op jit(solution)/shard_map/ppermute | solution.py:461
  54.6 6.9 %collective-permute-start.18 = (bf16[1,256,256]{2,1,0:T(8,128)(2,1)S(1)}, bf16[1,256,256]{2,1,0:T(8,128)(2,1)S(1)}, u32[]{:S(2)}, u32[]{:S(2)}) collective-permute-start(bf16[1,256,256]{2,1,0:T(8,128)(2,1)S(1)} %get-tuple-element.99), channel_id=1, source_target_pairs={{0,4},{4,0},{8,12},{12,8},{16,20},{20,16},{24,28},{28,24},{1,5},{5... | collective-permute-start | bytes 393224 | tf_op jit(solution)/shard_map/ppermute | solution.py:465
